TPU v7x, 32 devices: a whole 2x2x4 slice. The times are simulated.
32 devices in a mesh: groups: 2 (over x), dom: 16 (over z, y, core).
Axes of the slice: x: 2, y: 2, z: 4, core: 2. Of those that a mesh axis runs over, the one named last changes fastest.
Arguments:
- source: bfloat16 [72, 262144], P(None, ('groups', 'dom')), parts along dimension 1, may hold values from -6 to 6
- tile_weight: bfloat16 [8192, 128, 128], P('dom'), may hold values from -0.0625 to 0.0625
- tile_source: int32 [8192], P('dom'), may hold values from 0 to 127
- tile_slot: int32 [8192], P('dom'), may hold values from 0 to 15
- tile_count: int32 [16], P('dom'), may hold values from 64 to 512, as said below
- dest_block: int32 [256], P('dom'), may hold values from 0 to 63, as said below
- embed_weight: bfloat16 [1152, 1024], replicated, may hold values from -0.1875 to 0.1875
- embed_bias: float32 [1024], replicated, may hold values from -3 to 3
Outputs:
- remapped: bfloat16 [128, 72, 128], P(('groups', 'dom')), parts along dimension 0
- embedded: bfloat16 [1024, 1024], P(('groups', 'dom')), parts along dimension 0
There are 2 independent parts, one for each index of `groups`. A program takes and returns all parts, laid end to end along the dimension named above; an argument that names none is the same for every part. Nothing has to cross between parts.
Inputs may be any that keep to these rules, and one draw needn't show every extreme that they name: `tile_count`: number of live tiles of each device; the later tile slots are unused. Some device has all 512 tiles live. `dest_block`: the owner of target block b is device b // 4. Within one device's 16 entries the blocks are distinct and at most 2 of them belong to any one owner; on every device some owner has exactly 2.
All inputs are finite; a program needn't handle non-finite values.
Results may differ from a plain program's by a relative error of at most 0.0046.
Values may be sent and summed in bfloat16 or wider, within the bound.
No kernel may reach another device: no remote copies, remote signals or barrier semaphores. Data moves between devices by JAX's collectives and lax.ppermute only.
A program may use at most 128 MiB of HBM per device.

v0:
```python
import functools

import jax
import jax.numpy as jnp
from jax import lax
from jax.experimental import pallas as pl
from jax.experimental.pallas import tpu as pltpu
from jax.sharding import PartitionSpec as P

PATCH = 4
CAP = 2
TB_DEV = 4
LANES = 128
SEG = 4
UNROLL = 20
CHUNK = 64
VMEM = pl.BlockSpec(memory_space=pltpu.VMEM)
SMEM = pl.BlockSpec(memory_space=pltpu.SMEM)
ANY = pl.BlockSpec(memory_space=pl.ANY)


def up(n, step):
    return -(-n // step) * step


def list_rows(tiles, slots):
    entries = up(up(tiles + slots * (SEG - 1), SEG * UNROLL), LANES) // LANES
    return entries, -(-entries // SEG)


def iota(shape, dim):
    return lax.broadcasted_iota(jnp.int32, shape, dim)


def ones_of(mask):
    return jnp.where(mask, 1.0, 0.0)


def dot(a, b, dims):
    return lax.dot_general(
        a.astype(jnp.bfloat16),
        b.astype(jnp.bfloat16),
        (dims, ((), ())),
        preferred_element_type=jnp.float32,
    )


def store_row(out, row, values):
    for r in range(values.shape[1] // LANES):
        out[row + r : row + r + 1, :] = values[:, r * LANES : (r + 1) * LANES]


def schedule(block, slot, kinds, slots, outs):
    tiles = block.shape[1]
    bits = tiles.bit_length()
    entries, segments = list_rows(tiles, slots)
    bins = len(kinds) * slots
    slot_is = slot == iota((slots, tiles), 0)
    chosen = jnp.concatenate([ones_of(slot_is & kind) for kind in kinds], axis=0)
    before = ones_of(iota((tiles, tiles), 0) < iota((tiles, tiles), 1))
    rank = dot(chosen, before, ((1,), (0,)))
    total = jnp.sum(chosen, axis=1, keepdims=True).astype(jnp.int32)
    length = jnp.broadcast_to((total + (SEG - 1)) // SEG, (bins, LANES))
    a, b = iota((bins, bins), 0), iota((bins, bins), 1)
    upto = ones_of((b <= a) & (b // slots == a // slots))
    ends = dot(upto, length.astype(jnp.float32), ((1,), (0,))).astype(jnp.int32)
    begins = (ends - length)[:, :1] * SEG + iota((bins, 1), 0) // slots * (entries * LANES)
    place = jnp.sum(chosen * (rank + begins.astype(jnp.float32) + 1.0), axis=0, keepdims=True)
    place = place.astype(jnp.int32) - 1
    rows = up(len(kinds) * entries, 8)
    at_row = ones_of((place >> 7) == iota((rows, tiles), 0))
    at_lane = ones_of((place & (LANES - 1)) == iota((LANES, tiles), 0))
    count = tiles - iota((1, tiles), 1)
    values = [at_row * v.astype(jnp.float32) for v in (block, count >> 5, count & 31)]
    found = dot(jnp.concatenate(values, axis=0), at_lane, ((1,), (1,))).astype(jnp.int32)
    code = (found[:rows] << bits) | (found[rows : 2 * rows] << 5) | found[2 * rows :]
    for k, out in enumerate(outs):
        mine = ends[k * slots : (k + 1) * slots]
        out[:entries, :] = code[k * entries : (k + 1) * entries]
        passed = ones_of(mine[:, :1] <= iota((slots, segments * LANES), 1))
        owner = jnp.sum(passed, axis=0, keepdims=True).astype(jnp.int32)
        store_row(out, entries, jnp.minimum(owner, slots - 1))
        out[entries + segments : entries + segments + 1, :] = mine[slots - 1 :]


def slot_places(dest, me, members):
    slots = dest.shape[1]
    a, b = iota((slots, slots), 0), iota((slots, slots), 1)
    column = jnp.sum(jnp.where(a == b, dest.astype(jnp.float32), 0.0), axis=1, keepdims=True)
    column = column.astype(jnp.int32)
    owner = column // TB_DEV
    earlier = ones_of((owner == dest // TB_DEV) & (b < a))
    rank = jnp.sum(earlier, axis=1, keepdims=True).astype(jnp.int32)
    return owner & (members - 1), (owner // members) ^ (me // members), rank, column & (TB_DEV - 1)


def run_segments(tiles, slots, meta, x, w, acc):
    entries, segments = list_rows(tiles, slots)
    bits = tiles.bit_length()
    total = meta[entries + segments, 0]

    def step(i, carry):
        results = []
        for u in range(UNROLL):
            first = (i * UNROLL + u) * SEG
            row, lane = first >> 7, first & (LANES - 1)
            xs, ws = [], []
            for k in range(SEG):
                code = meta[row, lane + k]
                column = pl.multiple_of((code >> bits) * LANES, LANES)
                xs.append(x[:, pl.ds(column, LANES)])
                ws.append(w[tiles - (code & ((1 << bits) - 1))])
            results.append(
                jnp.dot(
                    jnp.concatenate(xs, axis=1),
                    jnp.concatenate(ws, axis=0),
                    preferred_element_type=jnp.float32,
                )
            )
        for u in range(UNROLL):
            g = i * UNROLL + u
            slot = meta[entries + (g >> 7), g & (LANES - 1)]
            acc[slot] += results[u]
        return carry

    lax.fori_loop(0, (total + UNROLL - 1) // UNROLL, step, 0)


def early_kernel(members, spans, me, count, *refs):
    tile_source, tile_slot, dest, source, near, weights, acc, held, late_list, *refs = refs
    labels, (x, ids, dests, lists, meta_a, meta_b, sems, weight_sems) = refs[: len(spans)], refs[len(spans) :]
    tiles, slots = tile_source.shape[1], dest.shape[1]
    cells = source.shape[1]
    live, me, core = count[0], me[0], me[0] & 1
    chunks = tiles // CHUNK

    def copy(c):
        part = pl.ds(c * CHUNK, CHUNK)
        return pltpu.make_async_copy(weights.at[part], held.at[part], weight_sems.at[c])

    ids_in = [
        pltpu.make_async_copy(tile_source, ids.at[0], sems.at[0]),
        pltpu.make_async_copy(tile_slot, ids.at[1], sems.at[1]),
        pltpu.make_async_copy(dest, dests, sems.at[6]),
    ]
    for c in ids_in:
        c.start()
    for c in range(chunks):
        pl.when(c * CHUNK < live)(lambda c=c: copy(c).start())
    half = cells // 2
    first = pl.multiple_of(core * half, LANES)
    cells_in = [
        pltpu.make_async_copy(source, x.at[:, pl.ds(0, cells)], sems.at[2]),
        pltpu.make_async_copy(near.at[:, pl.ds(first, half)], x.at[:, pl.ds(cells, half)], sems.at[3]),
    ]
    for c in cells_in:
        c.start()
    for c in ids_in:
        c.wait()

    own = cells // LANES
    rim = own // 2
    place = ids[0]
    on_left, on_right = place < rim, place >= rim + own
    inner = ~(on_left | on_right)
    at_hand = inner | (on_left & (core == 1)) | (on_right & (core == 0))
    offset = jnp.where(on_right, place - own - rim, place)
    block = jnp.where(inner, place - rim, jnp.where(at_hand, own + offset, offset))
    tile_ids = iota((1, tiles), 1)
    alive = tile_ids < live
    member, plane, rank, block_row = slot_places(dests[...], me, members)
    member = member ^ (me & (members - 1))
    kinds = [alive & at_hand & (tile_ids < tiles // 2), alive & at_hand & (tile_ids >= tiles // 2)]
    kinds += [alive & ~at_hand]
    schedule(block, ids[1], kinds, slots, (lists.at[0], lists.at[1], late_list))
    to_scalars = [
        pltpu.make_async_copy(lists.at[0], meta_a, sems.at[4]),
        pltpu.make_async_copy(lists.at[1], meta_b, sems.at[5]),
    ]
    for c in to_scalars:
        c.start()

    entries, segments = list_rows(tiles, slots)
    first, goes = 0, jnp.zeros((slots, 1), jnp.int32)
    for (lo, hi), label in zip(spans, labels):
        dense, rows = (hi - lo) * TB_DEV, (hi - lo) * CAP
        inside = (plane >= lo) & (plane < hi)
        spot = (plane - lo) * CAP + rank
        place = jnp.where(member == 0, (plane - lo) * TB_DEV + block_row, dense + (member - 1) * rows + spot)
        goes = jnp.where(inside, first + place, goes)
        first += dense + (members - 1) * rows
        for q in range(1, members):
            hit = inside & (member == q) & (spot == iota((slots, label.shape[1]), 1))
            found = dot(ones_of(hit), jnp.broadcast_to(block_row + 1, (slots, LANES)), ((0,), (0,)))
            label[q - 1] = (found - 1.0).astype(label.dtype)
    hit = goes == iota((slots, up(first, LANES)), 1)
    sources = jnp.sum(jnp.where(hit, (iota((slots, 1), 0) - slots).astype(jnp.float32), 0.0), axis=0, keepdims=True)
    store_row(late_list, entries + segments + 1, sources.astype(jnp.int32) + slots)

    acc[...] = jnp.zeros_like(acc)
    held[tiles] = jnp.zeros(held.shape[1:], held.dtype)
    for c in (*cells_in, *to_scalars):
        c.wait()
    for part, meta in ((0, meta_a), (1, meta_b)):
        for c in range(part * chunks // 2, (part + 1) * chunks // 2):
            pl.when(c * CHUNK < live)(lambda c=c: copy(c).wait())
        run_segments(tiles, slots, meta, x, held, acc)


def late_kernel(tiles, slots, members, meta, far, partial, held, *rest):
    n = (len(rest) - 1) // (members + 1)
    labels, outs, acc = rest[:n], rest[n:-1], rest[-1]
    acc[:slots] = partial[...]
    acc[slots] = jnp.zeros(acc.shape[1:], acc.dtype)
    run_segments(tiles, slots, meta, far, held, acc)
    spot = sum(list_rows(tiles, slots)) + 1
    p = 0

    def next_slot():
        nonlocal p
        p += 1
        return acc[meta[spot + (p - 1) // LANES, (p - 1) % LANES]]

    for i, label in enumerate(labels):
        own, *rows = outs[i * members : (i + 1) * members]
        dense, pair = own.shape[0], CAP * own.shape[1]
        planes = dense // TB_DEV
        for r in range(dense):
            own[r] = next_slot()
        for q, out in enumerate(rows):
            for m in range(planes):
                both = jnp.concatenate([next_slot() for _ in range(CAP)], axis=0)
                out[m * pair : (m + 1) * pair, :] = both.astype(out.dtype)
            out[planes * pair :, :] = label[q]


def plane_kernel(members, me, own, *refs):
    rows, outs = refs[: members - 1], refs[members - 1 :]
    dense, channels, cells = own.shape
    planes, pair = dense // TB_DEV, CAP * channels
    labels = [row[planes * pair :, :].astype(jnp.float32) for row in rows]
    for m in range(planes):
        sums = [own[m * TB_DEV + k] for k in range(TB_DEV)]
        for row, label in zip(rows, labels):
            both = row[m * pair : (m + 1) * pair, :].astype(jnp.float32)
            for c in range(CAP):
                value = both[c * channels : (c + 1) * channels]
                mark = jnp.broadcast_to(label[m * CAP + c : m * CAP + c + 1], (channels, cells))
                sums = [s + jnp.where(mark == k, value, 0.0) for k, s in enumerate(sums)]
        for k, s in enumerate(sums):
            if len(outs) == 1:
                outs[0][(me[0] ^ m) * TB_DEV + k] = s.astype(outs[0].dtype)
            else:
                outs[m][k] = s.astype(outs[m].dtype)


def final_kernel(choose, weight, bias, *refs):
    *parts, remapped, embedded, turned = refs
    blocks, channels, cells = remapped.shape
    for b in range(blocks):
        value = sum(p[i + b].astype(jnp.float32) for p in parts for i in range(0, p.shape[0], blocks))
        value = value.astype(jnp.bfloat16)
        remapped[b] = value
        turned[b] = lax.dot_general(
            choose[...], value, (((1,), (1,)), ((), ())), preferred_element_type=jnp.float32
        )
    per_block = cells // (PATCH * PATCH)
    total = jnp.broadcast_to(bias[...], (blocks * per_block, bias.shape[1]))
    for s in range(PATCH * PATCH):
        rows = turned[:, s * per_block : (s + 1) * per_block, :]
        rows = rows.reshape(blocks * per_block, channels).astype(jnp.bfloat16)
        total = total + jnp.dot(rows, weight[s], preferred_element_type=jnp.float32)
    embedded[...] = total.astype(jnp.bfloat16)


def chooser(cells):
    per_block = cells // (PATCH * PATCH)
    row = jnp.arange(cells, dtype=jnp.int32)
    r, q, p = row // (PATCH * per_block), row // per_block % PATCH, row % per_block
    wanted = r * (PATCH * per_block) + p * PATCH + q
    return (wanted[:, None] == jnp.arange(cells, dtype=jnp.int32)[None, :]).astype(jnp.bfloat16)


def in_vmem(x):
    return pltpu.with_memory_space_constraint(x, pltpu.VMEM)


def in_hbm(x):
    return pltpu.with_memory_space_constraint(x, pltpu.HBM)


def limit(mib):
    return pltpu.CompilerParams(vmem_limit_bytes=mib << 20)


def local(
    source, tile_weight, tile_source, tile_slot, tile_count, dest_block, embed_weight, embed_bias
):
    channels, own_cells = source.shape
    tiles, block_size, _ = tile_weight.shape
    slots = dest_block.shape[0]
    peers = lax.axis_size("dom")
    me = lax.axis_index("dom").astype(jnp.int32)
    core = me & 1
    width = own_cells // 2
    emb = embed_weight.shape[1]
    members = 4 if peers == 16 else 2
    planes = peers // members

    def swap(x, q):
        return lax.ppermute(x, "dom", [(i, i ^ q) for i in range(peers)])

    near = swap(source, 1)
    far = lax.ppermute(
        lax.dynamic_slice_in_dim(source, core * width, width, axis=1),
        "dom",
        [(i, (i + (1 if i % 2 else -1)) % peers) for i in range(peers)],
    )

    by_swap = planes == 4
    spans = ((0, 2), (2, 4)) if by_swap else ((0, planes),)
    entries, segments = list_rows(tiles, slots)

    def table(rows):
        return jax.ShapeDtypeStruct((up(rows, 8), LANES), jnp.int32)

    def label_shape(lo, hi):
        return (members - 1, up((hi - lo) * CAP, 16), LANES)

    acc_shape = (slots, channels, block_size)
    list_table = table(entries + segments + 1)
    map_rows = up(planes * (TB_DEV + (members - 1) * CAP), LANES) // LANES
    flops = tiles * channels * block_size * block_size
    partial, held, late_list, *labels = pl.pallas_call(
        functools.partial(early_kernel, members, spans),
        out_shape=(
            pltpu.VMEM(acc_shape, jnp.float32),
            pltpu.VMEM((tiles + 1, block_size, block_size), jnp.bfloat16),
            table(entries + segments + 1 + map_rows),
            *[jax.ShapeDtypeStruct(label_shape(*span), jnp.bfloat16) for span in spans],
        ),
        in_specs=[SMEM, SMEM] + [ANY] * 6,
        out_specs=(VMEM,) * (3 + len(spans)),
        scratch_shapes=[
            pltpu.VMEM((channels, own_cells + width), jnp.bfloat16),
            pltpu.VMEM((2, 1, tiles), jnp.int32),
            pltpu.VMEM((1, slots), jnp.int32),
            pltpu.VMEM((2, *list_table.shape), jnp.int32),
            pltpu.SMEM(list_table.shape, jnp.int32),
            pltpu.SMEM(list_table.shape, jnp.int32),
            pltpu.SemaphoreType.DMA((7,)),
            pltpu.SemaphoreType.DMA((tiles // CHUNK,)),
        ],
        compiler_params=limit(8),
        cost_estimate=pl.CostEstimate(
            flops=2 * flops, bytes_accessed=tile_weight.size * 2, transcendentals=0
        ),
        name="early_tiles",
    )(
        me[None],
        tile_count,
        in_hbm(tile_source[None, :]),
        in_hbm(tile_slot[None, :]),
        in_hbm(dest_block[None, :]),
        in_hbm(source),
        near,
        in_hbm(tile_weight),
    )

    area = PATCH * PATCH
    weight = embed_weight.reshape(channels, area, emb).transpose(1, 0, 2)

    cells = (channels, block_size)
    part = (TB_DEV, *cells)
    late_shapes = []
    for (lo, hi), label in zip(spans, labels):
        row_total = (hi - lo) * CAP * channels + label.shape[1]
        late_shapes.append(pltpu.VMEM(((hi - lo) * TB_DEV, *cells), jnp.float32))
        late_shapes += [jax.ShapeDtypeStruct((row_total, block_size), jnp.bfloat16)] * (members - 1)
    late = pl.pallas_call(
        functools.partial(late_kernel, tiles, slots, members),
        out_shape=tuple(late_shapes),
        in_specs=[SMEM] + [VMEM] * (3 + len(labels)),
        out_specs=(VMEM,) * len(late_shapes),
        scratch_shapes=[pltpu.VMEM((slots + 1, *cells), jnp.float32)],
        compiler_params=limit(6),
        cost_estimate=pl.CostEstimate(
            flops=flops, bytes_accessed=2 * channels * width, transcendentals=0
        ),
        name="late_tiles",
    )(late_list, far, in_vmem(partial), in_vmem(held), *labels)
    own_rows = []
    for i in range(len(spans)):
        own, *rows = late[i * members : (i + 1) * members]
        own_rows.append((own, [swap(r, q + 1) for q, r in enumerate(rows)]))

    parts = []
    for (lo, hi), (own, rows) in zip(spans, own_rows):
        if by_swap:
            part_shapes = [
                jax.ShapeDtypeStruct(part, jnp.bfloat16) if m else pltpu.VMEM(part, jnp.float32)
                for m in range(lo, hi)
            ]
        else:
            part_shapes = [jax.ShapeDtypeStruct(own.shape, jnp.bfloat16)]
        sums = pl.pallas_call(
            functools.partial(plane_kernel, members),
            out_shape=tuple(part_shapes),
            in_specs=[SMEM] + [VMEM] * members,
            out_specs=(VMEM,) * len(part_shapes),
            compiler_params=limit(4),
            name="plane_sum",
        )((me // members)[None], in_vmem(own), *rows)
        if by_swap:
            parts += [swap(s, m * members) if m else s for m, s in zip(range(lo, hi), sums)]
        else:
            columns = [[z * members + i for z in range(planes)] for i in range(members)]
            parts.append(lax.all_to_all(sums[0], "dom", 0, 0, tiled=True, axis_index_groups=columns))

    per_block = block_size // area
    return pl.pallas_call(
        final_kernel,
        out_shape=(
            jax.ShapeDtypeStruct(part, jnp.bfloat16),
            jax.ShapeDtypeStruct((TB_DEV * per_block, emb), jnp.bfloat16),
        ),
        in_specs=[VMEM] * (3 + len(parts)),
        out_specs=(VMEM, VMEM),
        scratch_shapes=[pltpu.VMEM((TB_DEV, block_size, channels), jnp.float32)],
        compiler_params=limit(6),
        name="embed",
    )(chooser(block_size), weight, embed_bias.reshape(1, emb), *parts)


def solution(mesh):
    placed = (
        P(None, ("groups", "dom")),
        P("dom", None, None),
        P("dom"),
        P("dom"),
        P("dom"),
        P("dom"),
        P(),
        P(),
    )
    return jax.shard_map(
        local,
        mesh=mesh,
        in_specs=placed,
        out_specs=(P(("groups", "dom"), None, None), P(("groups", "dom"), None)),
        check_vma=False,
    )
```

profile of v0, /device:TPU:0, one launch (start us, length us, event | category | flops | bytes accessed | tf_op | source)
XLA Modules:
  0.0 38.8 jit_solution(9501630317555376245)
XLA Ops:
  0.6 0.5 %collective-permute-start = (bf16[72,8192]{1,0:T(8,128)(2,1)}, bf16[72,8192]{1,0:T(8,128)(2,1)S(1)}, u32[]{:S(2)}, u32[]{:S(2)}) collective-permute-start(bf16[72,8192]{1,0:T(8,128)(2,1)} %refs_3_.1), channel_id=1, source_target_pairs={{0,1},{1,0},{2,3},{3,2},{4,5},{5,4},{6,7},{7,6},{8,9},{9,8},{10,11... | collective-permute-start | bytes 3538952 | tf_op jit(solution)/shard_map/ppermute | solution.py:311
  1.1 1.1 %constant_dynamic-slice_fusion = bf16[72,4096]{1,0:T(8,128)(2,1)S(1)} fusion(bf16[72,8192]{1,0:T(8,128)(2,1)} %refs_3_.1, s32[]{:T(128)S(6)} %select_n.48), kind=kLoop, calls=%fused_computation.19 | loop fusion | bytes 1179652 | tf_op jit(solution)/shard_map/dynamic_slice | solution.py:315
  2.3 5.7 %collective-permute-start.1 = (bf16[72,4096]{1,0:T(8,128)(2,1)S(1)}, bf16[72,4096]{1,0:T(8,128)(2,1)S(1)}, u32[]{:S(2)}, u32[]{:S(2)}) collective-permute-start(bf16[72,4096]{1,0:T(8,128)(2,1)S(1)} %constant_dynamic-slice_fusion), channel_id=1, source_target_pairs={{0,15},{1,2},{2,1},{3,4},{4,3},{5,6},{6,5},{7,8},{8,7},{9,10},{10,... | collective-permute-start | bytes 1769480 | tf_op jit(solution)/shard_map/ppermute | solution.py:314
  8.6 0.0 collective-permute-done.refs_4_
  8.6 3.5 %early_tiles.1 = (f32[16,72,128]{2,1,0:T(8,128)S(1)}, bf16[513,128,128]{2,1,0:T(8,128)(2,1)S(1)}, s32[16,128]{1,0:T(8,128)S(1)}, bf16[3,16,128]{2,1,0:T(8,128)(2,1)S(1)}, bf16[3,16,128]{2,1,0:T(8,128)(2,1)S(1)}) custom-call(s32[1]{0:T(128)} %bitcast.4.me, s32[1]{0:T(128)S(6)} %copy.13.count, s32[1,512]{1,0:T(1,128)} %bitcast.13, s32[1,512]{1,0:T(1,128)} %bitcast.14, ...), custom_call_target="tpu_custom_call" | custom-call | flops 1207959552 | bytes 16777216 | tf_op jit(solution)/shard_map/early_tiles/pallas_call | solution.py:334
  12.1 3.5 %collective-permute-done.1.far = bf16[72,4096]{1,0:T(8,128)(2,1)S(1)} collective-permute-done((bf16[72,4096]{1,0:T(8,128)(2,1)S(1)}, bf16[72,4096]{1,0:T(8,128)(2,1)S(1)}, u32[]{:S(2)}, u32[]{:S(2)}) %collective-permute-start.1) | collective-permute-done | bytes 589856 | tf_op jit(solution)/shard_map/ppermute | solution.py:314
  15.7 1.5 %late_tiles.1 = (f32[8,72,128]{2,1,0:T(8,128)S(1)}, bf16[304,128]{1,0:T(8,128)(2,1)S(1)}, bf16[304,128]{1,0:T(8,128)(2,1)S(1)}, bf16[304,128]{1,0:T(8,128)(2,1)S...) custom-call(s32[16,128]{1,0:T(8,128)S(1)} %get-tuple-element.19.meta, ...), custom_call_target="tpu_custom_call" | custom-call | flops 603979776 | bytes 589824 | tf_op jit(solution)/shard_map/late_tiles/pallas_call | solution.py:380
  17.2 3.3 %collective-permute-start.6 = (bf16[304,128]{1,0:T(8,128)(2,1)S(1)}, bf16[304,128]{1,0:T(8,128)(2,1)S(1)}, u32[]{:S(2)}, u32[]{:S(2)}) collective-permute-start(bf16[304,128]{1,0:T(8,128)(2,1)S(1)} %get-tuple-element.31), channel_id=1, source_target_pairs={{0,1},{1,0},{2,3},{3,2},{4,5},{5,4},{6,7},{7,6},{8,9},{9,8},{10,11... | collective-permute-start | bytes 233480 | tf_op jit(solution)/shard_map/ppermute | solution.py:311
  20.5 2.4 %collective-permute-start.7 = (bf16[304,128]{1,0:T(8,128)(2,1)S(1)}, bf16[304,128]{1,0:T(8,128)(2,1)S(1)}, u32[]{:S(2)}, u32[]{:S(2)}) collective-permute-start(bf16[304,128]{1,0:T(8,128)(2,1)S(1)} %get-tuple-element.32), channel_id=1, source_target_pairs={{0,2},{1,3},{2,0},{3,1},{4,6},{5,7},{6,4},{7,5},{8,10},{9,11},{10,... | collective-permute-start | bytes 233480 | tf_op jit(solution)/shard_map/ppermute | solution.py:311
  22.9 0.1 collective-permute-start.8
  22.9 0.2 collective-permute-start.2
  23.1 1.9 %collective-permute-start.3 = (bf16[304,128]{1,0:T(8,128)(2,1)S(1)}, bf16[304,128]{1,0:T(8,128)(2,1)S(1)}, u32[]{:S(2)}, u32[]{:S(2)}) collective-permute-start(bf16[304,128]{1,0:T(8,128)(2,1)S(1)} %get-tuple-element.26), channel_id=1, source_target_pairs={{0,2},{1,3},{2,0},{3,1},{4,6},{5,7},{6,4},{7,5},{8,10},{9,11},{10,... | collective-permute-start | bytes 233480 | tf_op jit(solution)/shard_map/ppermute | solution.py:311
  25.0 0.0 collective-permute-done.6.refs_0_
  25.0 0.0 collective-permute-start.4
  25.0 0.8 %collective-permute-done.7.refs_1_ = bf16[304,128]{1,0:T(8,128)(2,1)S(1)} collective-permute-done((bf16[304,128]{1,0:T(8,128)(2,1)S(1)}, bf16[304,128]{1,0:T(8,128)(2,1)S(1)}, u32[]{:S(2)}, u32[]{:S(2)}) %collective-permute-start.7) | collective-permute-done | bytes 77856 | tf_op jit(solution)/shard_map/ppermute | solution.py:311
  25.8 1.4 %collective-permute-done.8.refs_2_ = bf16[304,128]{1,0:T(8,128)(2,1)S(1)} collective-permute-done((bf16[304,128]{1,0:T(8,128)(2,1)S(1)}, bf16[304,128]{1,0:T(8,128)(2,1)S(1)}, u32[]{:S(2)}, u32[]{:S(2)}) %collective-permute-start.8) | collective-permute-done | bytes 77856 | tf_op jit(solution)/shard_map/ppermute | solution.py:311
  27.2 0.1 plane_sum.3
  27.4 3.2 %collective-permute-start.10 = (bf16[4,72,128]{2,1,0:T(8,128)(2,1)S(1)}, bf16[4,72,128]{2,1,0:T(8,128)(2,1)S(1)}, u32[]{:S(2)}, u32[]{:S(2)}) collective-permute-start(bf16[4,72,128]{2,1,0:T(8,128)(2,1)S(1)} %get-tuple-element.35), channel_id=1, source_target_pairs={{0,12},{1,13},{2,14},{3,15},{4,8},{5,9},{6,10},{7,11},{8,4},{9,5},... | collective-permute-start | bytes 221192 | tf_op jit(solution)/shard_map/ppermute | solution.py:311
  30.6 0.0 collective-permute-start.9
  30.6 0.0 collective-permute-done.2.refs_0_
  30.6 0.0 collective-permute-done.3.refs_1_
  30.6 0.0 collective-permute-done.4.refs_2_
  30.6 0.1 plane_sum.2
  30.8 1.3 %collective-permute-start.5 = (bf16[4,72,128]{2,1,0:T(8,128)(2,1)S(1)}, bf16[4,72,128]{2,1,0:T(8,128)(2,1)S(1)}, u32[]{:S(2)}, u32[]{:S(2)}) collective-permute-start(bf16[4,72,128]{2,1,0:T(8,128)(2,1)S(1)} %get-tuple-element.29), channel_id=1, source_target_pairs={{0,4},{1,5},{2,6},{3,7},{4,0},{5,1},{6,2},{7,3},{8,12},{9,13},{10,... | collective-permute-start | bytes 221192 | tf_op jit(solution)/shard_map/ppermute | solution.py:311
  32.1 0.1 fusion.choose
  32.2 0.0 copy-done.1
  32.2 0.0 copy-start
  32.2 1.3 %copy.12 = bf16[72,16,1024]{2,0,1:T(8,128)(2,1)S(1)} copy(bf16[72,16,1024]{2,1,0:T(8,128)(2,1)S(1)} %bitcast.12) | data formatting | bytes 4718592 | tf_op jit(solution)/shard_map/reshape | solution.py:371
  33.5 0.9 %collective-permute-done.10.refs_3_ = bf16[4,72,128]{2,1,0:T(8,128)(2,1)S(1)} collective-permute-done((bf16[4,72,128]{2,1,0:T(8,128)(2,1)S(1)}, bf16[4,72,128]{2,1,0:T(8,128)(2,1)S(1)}, u32[]{:S(2)}, u32[]{:S(2)}) %collective-permute-start.10) | collective-permute-done | bytes 73760 | tf_op jit(solution)/shard_map/ppermute | solution.py:311
  34.4 3.1 %collective-permute-done.9.refs_2_ = bf16[4,72,128]{2,1,0:T(8,128)(2,1)S(1)} collective-permute-done((bf16[4,72,128]{2,1,0:T(8,128)(2,1)S(1)}, bf16[4,72,128]{2,1,0:T(8,128)(2,1)S(1)}, u32[]{:S(2)}, u32[]{:S(2)}) %collective-permute-start.9) | collective-permute-done | bytes 73760 | tf_op jit(solution)/shard_map/ppermute | solution.py:311
  37.5 0.0 collective-permute-done.5.refs_1_
  37.5 1.3 %embed.1 = (bf16[4,72,128]{2,1,0:T(8,128)(2,1)}, bf16[32,1024]{1,0:T(8,128)(2,1)}) custom-call(bf16[128,128]{1,0:T(8,128)(2,1)S(1)} %fusion.choose, bf16[16,72,1024]{2,1,0:T(8,128)(2,1)S(1)} %bitcast.10, f32[1,1024]{1,0:T(1,128)S(1)} %bitcast.11, f32[4,72,128]{2,1,0:T(8,128)S(1)} %get-tuple-element.28.refs_0_, ...), custom_call_target="tpu_custom_call" | custom-call | tf_op jit(solution)/shard_map/embed/pallas_call | solution.py:421
  (3 shorter events, 0.0 us)
Async XLA Ops:
  0.6 8.0 %collective-permute-start = (bf16[72,8192]{1,0:T(8,128)(2,1)}, bf16[72,8192]{1,0:T(8,128)(2,1)S(1)}, u32[]{:S(2)}, u32[]{:S(2)}) collective-permute-start(bf16[72,8192]{1,0:T(8,128)(2,1)} %refs_3_.1), channel_id=1, source_target_pairs={{0,1},{1,0},{2,3},{3,2},{4,5},{5,4},{6,7},{7,6},{8,9},{9,8},{10,11... | collective-permute-start | bytes 3538952 | tf_op jit(solution)/shard_map/ppermute | solution.py:311
  2.3 13.4 %collective-permute-start.1 = (bf16[72,4096]{1,0:T(8,128)(2,1)S(1)}, bf16[72,4096]{1,0:T(8,128)(2,1)S(1)}, u32[]{:S(2)}, u32[]{:S(2)}) collective-permute-start(bf16[72,4096]{1,0:T(8,128)(2,1)S(1)} %constant_dynamic-slice_fusion), channel_id=1, source_target_pairs={{0,15},{1,2},{2,1},{3,4},{4,3},{5,6},{6,5},{7,8},{8,7},{9,10},{10,... | collective-permute-start | bytes 1769480 | tf_op jit(solution)/shard_map/ppermute | solution.py:314
  15.7 16.5 %copy-start.1 = (bf16[1152,1024]{1,0:T(8,128)(2,1)S(1)}, bf16[1152,1024]{1,0:T(8,128)(2,1)}, u32[]{:S(2)}) copy-start(bf16[1152,1024]{1,0:T(8,128)(2,1)} %param.14) | copy-start | bytes 7077892
  17.2 7.8 %collective-permute-start.6 = (bf16[304,128]{1,0:T(8,128)(2,1)S(1)}, bf16[304,128]{1,0:T(8,128)(2,1)S(1)}, u32[]{:S(2)}, u32[]{:S(2)}) collective-permute-start(bf16[304,128]{1,0:T(8,128)(2,1)S(1)} %get-tuple-element.31), channel_id=1, source_target_pairs={{0,1},{1,0},{2,3},{3,2},{4,5},{5,4},{6,7},{7,6},{8,9},{9,8},{10,11... | collective-permute-start | bytes 233480 | tf_op jit(solution)/shard_map/ppermute | solution.py:311
  20.5 5.3 %collective-permute-start.7 = (bf16[304,128]{1,0:T(8,128)(2,1)S(1)}, bf16[304,128]{1,0:T(8,128)(2,1)S(1)}, u32[]{:S(2)}, u32[]{:S(2)}) collective-permute-start(bf16[304,128]{1,0:T(8,128)(2,1)S(1)} %get-tuple-element.32), channel_id=1, source_target_pairs={{0,2},{1,3},{2,0},{3,1},{4,6},{5,7},{6,4},{7,5},{8,10},{9,11},{10,... | collective-permute-start | bytes 233480 | tf_op jit(solution)/shard_map/ppermute | solution.py:311
  22.9 4.4 %collective-permute-start.8 = (bf16[304,128]{1,0:T(8,128)(2,1)S(1)}, bf16[304,128]{1,0:T(8,128)(2,1)S(1)}, u32[]{:S(2)}, u32[]{:S(2)}) collective-permute-start(bf16[304,128]{1,0:T(8,128)(2,1)S(1)} %get-tuple-element.33), channel_id=1, source_target_pairs={{0,3},{1,2},{2,1},{3,0},{4,7},{5,6},{6,5},{7,4},{8,11},{9,10},{10,... | collective-permute-start | bytes 233480 | tf_op jit(solution)/shard_map/ppermute | solution.py:311
  22.9 7.7 %collective-permute-start.2 = (bf16[304,128]{1,0:T(8,128)(2,1)S(1)}, bf16[304,128]{1,0:T(8,128)(2,1)S(1)}, u32[]{:S(2)}, u32[]{:S(2)}) collective-permute-start(bf16[304,128]{1,0:T(8,128)(2,1)S(1)} %get-tuple-element.25), channel_id=1, source_target_pairs={{0,1},{1,0},{2,3},{3,2},{4,5},{5,4},{6,7},{7,6},{8,9},{9,8},{10,11... | collective-permute-start | bytes 233480 | tf_op jit(solution)/shard_map/ppermute | solution.py:311
  23.1 7.5 %collective-permute-start.3 = (bf16[304,128]{1,0:T(8,128)(2,1)S(1)}, bf16[304,128]{1,0:T(8,128)(2,1)S(1)}, u32[]{:S(2)}, u32[]{:S(2)}) collective-permute-start(bf16[304,128]{1,0:T(8,128)(2,1)S(1)} %get-tuple-element.26), channel_id=1, source_target_pairs={{0,2},{1,3},{2,0},{3,1},{4,6},{5,7},{6,4},{7,5},{8,10},{9,11},{10,... | collective-permute-start | bytes 233480 | tf_op jit(solution)/shard_map/ppermute | solution.py:311
  25.0 5.6 %collective-permute-start.4 = (bf16[304,128]{1,0:T(8,128)(2,1)S(1)}, bf16[304,128]{1,0:T(8,128)(2,1)S(1)}, u32[]{:S(2)}, u32[]{:S(2)}) collective-permute-start(bf16[304,128]{1,0:T(8,128)(2,1)S(1)} %get-tuple-element.27), channel_id=1, source_target_pairs={{0,3},{1,2},{2,1},{3,0},{4,7},{5,6},{6,5},{7,4},{8,11},{9,10},{10,... | collective-permute-start | bytes 233480 | tf_op jit(solution)/shard_map/ppermute | solution.py:311
  27.4 7.0 %collective-permute-start.10 = (bf16[4,72,128]{2,1,0:T(8,128)(2,1)S(1)}, bf16[4,72,128]{2,1,0:T(8,128)(2,1)S(1)}, u32[]{:S(2)}, u32[]{:S(2)}) collective-permute-start(bf16[4,72,128]{2,1,0:T(8,128)(2,1)S(1)} %get-tuple-element.35), channel_id=1, source_target_pairs={{0,12},{1,13},{2,14},{3,15},{4,8},{5,9},{6,10},{7,11},{8,4},{9,5},... | collective-permute-start | bytes 221192 | tf_op jit(solution)/shard_map/ppermute | solution.py:311
  30.6 6.9 %collective-permute-start.9 = (bf16[4,72,128]{2,1,0:T(8,128)(2,1)S(1)}, bf16[4,72,128]{2,1,0:T(8,128)(2,1)S(1)}, u32[]{:S(2)}, u32[]{:S(2)}) collective-permute-start(bf16[4,72,128]{2,1,0:T(8,128)(2,1)S(1)} %get-tuple-element.34), channel_id=1, source_target_pairs={{0,8},{1,9},{2,10},{3,11},{4,12},{5,13},{6,14},{7,15},{8,0},{9,1},... | collective-permute-start | bytes 221192 | tf_op jit(solution)/shard_map/ppermute | solution.py:311
  30.8 6.7 %collective-permute-start.5 = (bf16[4,72,128]{2,1,0:T(8,128)(2,1)S(1)}, bf16[4,72,128]{2,1,0:T(8,128)(2,1)S(1)}, u32[]{:S(2)}, u32[]{:S(2)}) collective-permute-start(bf16[4,72,128]{2,1,0:T(8,128)(2,1)S(1)} %get-tuple-element.29), channel_id=1, source_target_pairs={{0,4},{1,5},{2,6},{3,7},{4,0},{5,1},{6,2},{7,3},{8,12},{9,13},{10,... | collective-permute-start | bytes 221192 | tf_op jit(solution)/shard_map/ppermute | solution.py:311
  32.2 5.3 %copy-start = (f32[1024]{0:T(1024)S(1)}, f32[1024]{0:T(1024)}, u32[]{:S(2)}) copy-start(f32[1024]{0:T(1024)} %param.15) | copy-start | bytes 12292
where the time goes:
time: 39 us; the launch traced here: 38.8 us
  starting transfers between devices  18.6 us (48%)
  waiting for transfers between devices  9.75 us (25%)
  Pallas kernels  6.58 us (17%)
  local copies, waits for them, and re-layouts  2.41 us (6%)
  between operations  1.36 us (3%)
    ppermute x10, starting transfers between devices, swap(): return lax.ppermute(x, 'dom', [(i, i ^ q) for i in range(peers)])  12.9 us
    ppermute x10, waiting for transfers between devices, swap(): return lax.ppermute(x, 'dom', [(i, i ^ q) for i in range(peers)])  6.21 us
    ppermute x1, starting transfers between devices, local(): lax.ppermute(lax.dynamic_slice_in_dim(source, core * width, width, axis=1...  5.73 us
    ppermute x1, waiting for transfers between devices, local(): lax.ppermute(lax.dynamic_slice_in_dim(source, core * width, width, axis=1...  3.54 us
    pallas_call x1, Pallas kernels, local(): pl.pallas_call(functools.partial(early_kernel, members, spans), out_shape...  3.47 us
    pallas_call x1, Pallas kernels, local(): pl.pallas_call(functools.partial(late_kernel, tiles, slots, members), out...  1.51 us
    pallas_call x1, Pallas kernels, local(): pl.pallas_call(final_kernel, out_shape=(jax.ShapeDtypeStruct(part, jnp.bf...  1.3 us
    reshape x1, local copies, waits for them, and re-layouts, local(): weight = embed_weight.reshape(channels, area, emb).transpose(1, 0, 2)  1.3 us
  transfers between devices with their start and end apart: 11, of which 5 were waited for; matrix products, arithmetic and copies ran while one was open for 6% of the time, Pallas kernels for 10%

commit v1 on v0

--- a/solution.py
+++ b/solution.py
@@ -392,7 +392,8 @@
     own_rows = []
     for i in range(len(spans)):
         own, *rows = late[i * members : (i + 1) * members]
-        own_rows.append((own, [swap(r, q + 1) for q, r in enumerate(rows)]))
+        swapped = [swap(r, q + 1) for q, r in enumerate(rows)]
+        own_rows.append((own, swapped[1:] + swapped[:1]))
 
     parts = []
     for (lo, hi), (own, rows) in zip(spans, own_rows):

time: 39 us -> 39.2 us (level)
  waiting for transfers between devices: 9.75 us -> 8.29 us
  Pallas kernels: 6.58 us -> 7.94 us
  starting transfers between devices: 18.6 us -> 19 us
    ppermute x1, waiting for transfers between devices: 3.54 us -> 2.18 us  [local(): lax.ppermute(lax.dynamic_slice_in_dim(source, core * width, width, axis=1...]
    pallas_call x1, Pallas kernels: 3.47 us -> 4.83 us  [local(): pl.pallas_call(functools.partial(early_kernel, members, spans), out_shape...]
  transfers between devices with their start and end apart: 11 -> 11, of which waited for: 5 -> 4; matrix products, arithmetic and copies ran while one was open for 6% -> 6% of each run, Pallas kernels for 10% -> 13%
where the time goes in v1:
time: 39.2 us; the launch traced here: 39.1 us
  starting transfers between devices  19 us (48%)
  waiting for transfers between devices  8.29 us (21%)
  Pallas kernels  7.94 us (20%)
  local copies, waits for them, and re-layouts  2.41 us (6%)
  between operations  1.37 us (3%)
    ppermute x10, starting transfers between devices, swap(): return lax.ppermute(x, 'dom', [(i, i ^ q) for i in range(peers)])  13.2 us
    ppermute x10, waiting for transfers between devices, swap(): return lax.ppermute(x, 'dom', [(i, i ^ q) for i in range(peers)])  6.11 us
    ppermute x1, starting transfers between devices, local(): lax.ppermute(lax.dynamic_slice_in_dim(source, core * width, width, axis=1...  5.73 us
    pallas_call x1, Pallas kernels, local(): pl.pallas_call(functools.partial(early_kernel, members, spans), out_shape...  4.83 us
    ppermute x1, waiting for transfers between devices, local(): lax.ppermute(lax.dynamic_slice_in_dim(source, core * width, width, axis=1...  2.18 us
    pallas_call x1, Pallas kernels, local(): pl.pallas_call(functools.partial(late_kernel, tiles, slots, members), out...  1.51 us
    pallas_call x1, Pallas kernels, local(): pl.pallas_call(final_kernel, out_shape=(jax.ShapeDtypeStruct(part, jnp.bf...  1.3 us
    reshape x1, local copies, waits for them, and re-layouts, local(): weight = embed_weight.reshape(channels, area, emb).transpose(1, 0, 2)  1.3 us
  transfers between devices with their start and end apart: 11, of which 4 were waited for; matrix products, arithmetic and copies ran while one was open for 6% of the time, Pallas kernels for 13%

profile of v1, /device:TPU:0, one launch (start us, length us, event | category | flops | bytes accessed | tf_op | source)
XLA Modules:
  0.0 39.1 jit_solution(8442896115709365360)
XLA Ops:
  0.6 0.5 %collective-permute-start = (bf16[72,8192]{1,0:T(8,128)(2,1)}, bf16[72,8192]{1,0:T(8,128)(2,1)S(1)}, u32[]{:S(2)}, u32[]{:S(2)}) collective-permute-start(bf16[72,8192]{1,0:T(8,128)(2,1)} %refs_3_.1), channel_id=1, source_target_pairs={{0,1},{1,0},{2,3},{3,2},{4,5},{5,4},{6,7},{7,6},{8,9},{9,8},{10,11... | collective-permute-start | bytes 3538952 | tf_op jit(solution)/shard_map/ppermute | solution.py:311
  1.1 1.1 %constant_dynamic-slice_fusion = bf16[72,4096]{1,0:T(8,128)(2,1)S(1)} fusion(bf16[72,8192]{1,0:T(8,128)(2,1)} %refs_3_.1, s32[]{:T(128)S(6)} %select_n.48), kind=kLoop, calls=%fused_computation.19 | loop fusion | bytes 1179652 | tf_op jit(solution)/shard_map/dynamic_slice | solution.py:315
  2.3 5.7 %collective-permute-start.1 = (bf16[72,4096]{1,0:T(8,128)(2,1)S(1)}, bf16[72,4096]{1,0:T(8,128)(2,1)S(1)}, u32[]{:S(2)}, u32[]{:S(2)}) collective-permute-start(bf16[72,4096]{1,0:T(8,128)(2,1)S(1)} %constant_dynamic-slice_fusion), channel_id=1, source_target_pairs={{0,15},{1,2},{2,1},{3,4},{4,3},{5,6},{6,5},{7,8},{8,7},{9,10},{10,... | collective-permute-start | bytes 1769480 | tf_op jit(solution)/shard_map/ppermute | solution.py:314
  8.6 0.0 collective-permute-done.refs_4_
  8.6 4.8 %early_tiles.1 = (f32[16,72,128]{2,1,0:T(8,128)S(1)}, bf16[513,128,128]{2,1,0:T(8,128)(2,1)S(1)}, s32[16,128]{1,0:T(8,128)S(1)}, bf16[3,16,128]{2,1,0:T(8,128)(2,1)S(1)}, bf16[3,16,128]{2,1,0:T(8,128)(2,1)S(1)}) custom-call(s32[1]{0:T(128)} %bitcast.4.me, s32[1]{0:T(128)S(6)} %copy.13.count, s32[1,512]{1,0:T(1,128)} %bitcast.13, s32[1,512]{1,0:T(1,128)} %bitcast.14, ...), custom_call_target="tpu_custom_call" | custom-call | flops 1207959552 | bytes 16777216 | tf_op jit(solution)/shard_map/early_tiles/pallas_call | solution.py:334
  13.5 2.2 %collective-permute-done.1.far = bf16[72,4096]{1,0:T(8,128)(2,1)S(1)} collective-permute-done((bf16[72,4096]{1,0:T(8,128)(2,1)S(1)}, bf16[72,4096]{1,0:T(8,128)(2,1)S(1)}, u32[]{:S(2)}, u32[]{:S(2)}) %collective-permute-start.1) | collective-permute-done | bytes 589856 | tf_op jit(solution)/shard_map/ppermute | solution.py:314
  15.7 1.5 %late_tiles.1 = (f32[8,72,128]{2,1,0:T(8,128)S(1)}, bf16[304,128]{1,0:T(8,128)(2,1)S(1)}, bf16[304,128]{1,0:T(8,128)(2,1)S(1)}, bf16[304,128]{1,0:T(8,128)(2,1)S...) custom-call(s32[16,128]{1,0:T(8,128)S(1)} %get-tuple-element.19.meta, ...), custom_call_target="tpu_custom_call" | custom-call | flops 603979776 | bytes 589824 | tf_op jit(solution)/shard_map/late_tiles/pallas_call | solution.py:380
  17.2 4.9 %collective-permute-start.6 = (bf16[304,128]{1,0:T(8,128)(2,1)S(1)}, bf16[304,128]{1,0:T(8,128)(2,1)S(1)}, u32[]{:S(2)}, u32[]{:S(2)}) collective-permute-start(bf16[304,128]{1,0:T(8,128)(2,1)S(1)} %get-tuple-element.31), channel_id=1, source_target_pairs={{0,2},{1,3},{2,0},{3,1},{4,6},{5,7},{6,4},{7,5},{8,10},{9,11},{10,... | collective-permute-start | bytes 233480 | tf_op jit(solution)/shard_map/ppermute | solution.py:311
  22.1 0.0 collective-permute-start.7
  22.1 0.2 collective-permute-start.8
  22.3 1.9 %collective-permute-start.2 = (bf16[304,128]{1,0:T(8,128)(2,1)S(1)}, bf16[304,128]{1,0:T(8,128)(2,1)S(1)}, u32[]{:S(2)}, u32[]{:S(2)}) collective-permute-start(bf16[304,128]{1,0:T(8,128)(2,1)S(1)} %get-tuple-element.25), channel_id=1, source_target_pairs={{0,2},{1,3},{2,0},{3,1},{4,6},{5,7},{6,4},{7,5},{8,10},{9,11},{10,... | collective-permute-start | bytes 233480 | tf_op jit(solution)/shard_map/ppermute | solution.py:311
  24.2 0.0 collective-permute-start.3
  24.2 0.5 %collective-permute-done.6.refs_0_ = bf16[304,128]{1,0:T(8,128)(2,1)S(1)} collective-permute-done((bf16[304,128]{1,0:T(8,128)(2,1)S(1)}, bf16[304,128]{1,0:T(8,128)(2,1)S(1)}, u32[]{:S(2)}, u32[]{:S(2)}) %collective-permute-start.6) | collective-permute-done | bytes 77856 | tf_op jit(solution)/shard_map/ppermute | solution.py:311
  24.7 0.0 collective-permute-start.4
  24.7 2.1 %collective-permute-done.7.refs_1_ = bf16[304,128]{1,0:T(8,128)(2,1)S(1)} collective-permute-done((bf16[304,128]{1,0:T(8,128)(2,1)S(1)}, bf16[304,128]{1,0:T(8,128)(2,1)S(1)}, u32[]{:S(2)}, u32[]{:S(2)}) %collective-permute-start.7) | collective-permute-done | bytes 77856 | tf_op jit(solution)/shard_map/ppermute | solution.py:311
  26.8 0.0 collective-permute-done.8.refs_2_
  26.8 0.1 plane_sum.3
  27.0 4.0 %collective-permute-start.10 = (bf16[4,72,128]{2,1,0:T(8,128)(2,1)S(1)}, bf16[4,72,128]{2,1,0:T(8,128)(2,1)S(1)}, u32[]{:S(2)}, u32[]{:S(2)}) collective-permute-start(bf16[4,72,128]{2,1,0:T(8,128)(2,1)S(1)} %get-tuple-element.35), channel_id=1, source_target_pairs={{0,12},{1,13},{2,14},{3,15},{4,8},{5,9},{6,10},{7,11},{8,4},{9,5},... | collective-permute-start | bytes 221192 | tf_op jit(solution)/shard_map/ppermute | solution.py:311
  31.0 0.3 collective-permute-start.9
  31.3 0.0 collective-permute-done.2.refs_0_
  31.3 0.0 collective-permute-done.3.refs_1_
  31.3 0.0 collective-permute-done.4.refs_2_
  31.3 0.1 plane_sum.2
  31.5 1.3 %collective-permute-start.5 = (bf16[4,72,128]{2,1,0:T(8,128)(2,1)S(1)}, bf16[4,72,128]{2,1,0:T(8,128)(2,1)S(1)}, u32[]{:S(2)}, u32[]{:S(2)}) collective-permute-start(bf16[4,72,128]{2,1,0:T(8,128)(2,1)S(1)} %get-tuple-element.29), channel_id=1, source_target_pairs={{0,4},{1,5},{2,6},{3,7},{4,0},{5,1},{6,2},{7,3},{8,12},{9,13},{10,... | collective-permute-start | bytes 221192 | tf_op jit(solution)/shard_map/ppermute | solution.py:311
  32.8 0.1 fusion.choose
  32.9 0.0 copy-done.1
  32.9 0.0 copy-start
  32.9 1.3 %copy.12 = bf16[72,16,1024]{2,0,1:T(8,128)(2,1)S(1)} copy(bf16[72,16,1024]{2,1,0:T(8,128)(2,1)S(1)} %bitcast.12) | data formatting | bytes 4718592 | tf_op jit(solution)/shard_map/reshape | solution.py:371
  34.2 0.0 collective-permute-done.10.refs_3_
  34.2 3.5 %collective-permute-done.9.refs_2_ = bf16[4,72,128]{2,1,0:T(8,128)(2,1)S(1)} collective-permute-done((bf16[4,72,128]{2,1,0:T(8,128)(2,1)S(1)}, bf16[4,72,128]{2,1,0:T(8,128)(2,1)S(1)}, u32[]{:S(2)}, u32[]{:S(2)}) %collective-permute-start.9) | collective-permute-done | bytes 73760 | tf_op jit(solution)/shard_map/ppermute | solution.py:311
  37.8 0.0 collective-permute-done.5.refs_1_
  37.8 1.3 %embed.1 = (bf16[4,72,128]{2,1,0:T(8,128)(2,1)}, bf16[32,1024]{1,0:T(8,128)(2,1)}) custom-call(bf16[128,128]{1,0:T(8,128)(2,1)S(1)} %fusion.choose, bf16[16,72,1024]{2,1,0:T(8,128)(2,1)S(1)} %bitcast.10, f32[1,1024]{1,0:T(1,128)S(1)} %bitcast.11, f32[4,72,128]{2,1,0:T(8,128)S(1)} %get-tuple-element.28.refs_0_, ...), custom_call_target="tpu_custom_call" | custom-call | tf_op jit(solution)/shard_map/embed/pallas_call | solution.py:422
  (3 shorter events, 0.0 us)
Async XLA Ops:
  0.6 8.0 %collective-permute-start = (bf16[72,8192]{1,0:T(8,128)(2,1)}, bf16[72,8192]{1,0:T(8,128)(2,1)S(1)}, u32[]{:S(2)}, u32[]{:S(2)}) collective-permute-start(bf16[72,8192]{1,0:T(8,128)(2,1)} %refs_3_.1), channel_id=1, source_target_pairs={{0,1},{1,0},{2,3},{3,2},{4,5},{5,4},{6,7},{7,6},{8,9},{9,8},{10,11... | collective-permute-start | bytes 3538952 | tf_op jit(solution)/shard_map/ppermute | solution.py:311
  2.3 13.4 %collective-permute-start.1 = (bf16[72,4096]{1,0:T(8,128)(2,1)S(1)}, bf16[72,4096]{1,0:T(8,128)(2,1)S(1)}, u32[]{:S(2)}, u32[]{:S(2)}) collective-permute-start(bf16[72,4096]{1,0:T(8,128)(2,1)S(1)} %constant_dynamic-slice_fusion), channel_id=1, source_target_pairs={{0,15},{1,2},{2,1},{3,4},{4,3},{5,6},{6,5},{7,8},{8,7},{9,10},{10,... | collective-permute-start | bytes 1769480 | tf_op jit(solution)/shard_map/ppermute | solution.py:314
  15.7 17.2 %copy-start.1 = (bf16[1152,1024]{1,0:T(8,128)(2,1)S(1)}, bf16[1152,1024]{1,0:T(8,128)(2,1)}, u32[]{:S(2)}) copy-start(bf16[1152,1024]{1,0:T(8,128)(2,1)} %param.14) | copy-start | bytes 7077892
  17.2 7.5 %collective-permute-start.6 = (bf16[304,128]{1,0:T(8,128)(2,1)S(1)}, bf16[304,128]{1,0:T(8,128)(2,1)S(1)}, u32[]{:S(2)}, u32[]{:S(2)}) collective-permute-start(bf16[304,128]{1,0:T(8,128)(2,1)S(1)} %get-tuple-element.31), channel_id=1, source_target_pairs={{0,2},{1,3},{2,0},{3,1},{4,6},{5,7},{6,4},{7,5},{8,10},{9,11},{10,... | collective-permute-start | bytes 233480 | tf_op jit(solution)/shard_map/ppermute | solution.py:311
  22.1 4.7 %collective-permute-start.7 = (bf16[304,128]{1,0:T(8,128)(2,1)S(1)}, bf16[304,128]{1,0:T(8,128)(2,1)S(1)}, u32[]{:S(2)}, u32[]{:S(2)}) collective-permute-start(bf16[304,128]{1,0:T(8,128)(2,1)S(1)} %get-tuple-element.32), channel_id=1, source_target_pairs={{0,3},{1,2},{2,1},{3,0},{4,7},{5,6},{6,5},{7,4},{8,11},{9,10},{10,... | collective-permute-start | bytes 233480 | tf_op jit(solution)/shard_map/ppermute | solution.py:311
  22.1 4.7 %collective-permute-start.8 = (bf16[304,128]{1,0:T(8,128)(2,1)S(1)}, bf16[304,128]{1,0:T(8,128)(2,1)S(1)}, u32[]{:S(2)}, u32[]{:S(2)}) collective-permute-start(bf16[304,128]{1,0:T(8,128)(2,1)S(1)} %get-tuple-element.33), channel_id=1, source_target_pairs={{0,1},{1,0},{2,3},{3,2},{4,5},{5,4},{6,7},{7,6},{8,9},{9,8},{10,11... | collective-permute-start | bytes 233480 | tf_op jit(solution)/shard_map/ppermute | solution.py:311
  22.3 9.0 %collective-permute-start.2 = (bf16[304,128]{1,0:T(8,128)(2,1)S(1)}, bf16[304,128]{1,0:T(8,128)(2,1)S(1)}, u32[]{:S(2)}, u32[]{:S(2)}) collective-permute-start(bf16[304,128]{1,0:T(8,128)(2,1)S(1)} %get-tuple-element.25), channel_id=1, source_target_pairs={{0,2},{1,3},{2,0},{3,1},{4,6},{5,7},{6,4},{7,5},{8,10},{9,11},{10,... | collective-permute-start | bytes 233480 | tf_op jit(solution)/shard_map/ppermute | solution.py:311
  24.2 7.1 %collective-permute-start.3 = (bf16[304,128]{1,0:T(8,128)(2,1)S(1)}, bf16[304,128]{1,0:T(8,128)(2,1)S(1)}, u32[]{:S(2)}, u32[]{:S(2)}) collective-permute-start(bf16[304,128]{1,0:T(8,128)(2,1)S(1)} %get-tuple-element.26), channel_id=1, source_target_pairs={{0,3},{1,2},{2,1},{3,0},{4,7},{5,6},{6,5},{7,4},{8,11},{9,10},{10,... | collective-permute-start | bytes 233480 | tf_op jit(solution)/shard_map/ppermute | solution.py:311
  24.7 6.6 %collective-permute-start.4 = (bf16[304,128]{1,0:T(8,128)(2,1)S(1)}, bf16[304,128]{1,0:T(8,128)(2,1)S(1)}, u32[]{:S(2)}, u32[]{:S(2)}) collective-permute-start(bf16[304,128]{1,0:T(8,128)(2,1)S(1)} %get-tuple-element.27), channel_id=1, source_target_pairs={{0,1},{1,0},{2,3},{3,2},{4,5},{5,4},{6,7},{7,6},{8,9},{9,8},{10,11... | collective-permute-start | bytes 233480 | tf_op jit(solution)/shard_map/ppermute | solution.py:311
  27.0 7.3 %collective-permute-start.10 = (bf16[4,72,128]{2,1,0:T(8,128)(2,1)S(1)}, bf16[4,72,128]{2,1,0:T(8,128)(2,1)S(1)}, u32[]{:S(2)}, u32[]{:S(2)}) collective-permute-start(bf16[4,72,128]{2,1,0:T(8,128)(2,1)S(1)} %get-tuple-element.35), channel_id=1, source_target_pairs={{0,12},{1,13},{2,14},{3,15},{4,8},{5,9},{6,10},{7,11},{8,4},{9,5},... | collective-permute-start | bytes 221192 | tf_op jit(solution)/shard_map/ppermute | solution.py:311
  31.0 6.8 %collective-permute-start.9 = (bf16[4,72,128]{2,1,0:T(8,128)(2,1)S(1)}, bf16[4,72,128]{2,1,0:T(8,128)(2,1)S(1)}, u32[]{:S(2)}, u32[]{:S(2)}) collective-permute-start(bf16[4,72,128]{2,1,0:T(8,128)(2,1)S(1)} %get-tuple-element.34), channel_id=1, source_target_pairs={{0,8},{1,9},{2,10},{3,11},{4,12},{5,13},{6,14},{7,15},{8,0},{9,1},... | collective-permute-start | bytes 221192 | tf_op jit(solution)/shard_map/ppermute | solution.py:311
  31.5 6.3 %collective-permute-start.5 = (bf16[4,72,128]{2,1,0:T(8,128)(2,1)S(1)}, bf16[4,72,128]{2,1,0:T(8,128)(2,1)S(1)}, u32[]{:S(2)}, u32[]{:S(2)}) collective-permute-start(bf16[4,72,128]{2,1,0:T(8,128)(2,1)S(1)} %get-tuple-element.29), channel_id=1, source_target_pairs={{0,4},{1,5},{2,6},{3,7},{4,0},{5,1},{6,2},{7,3},{8,12},{9,13},{10,... | collective-permute-start | bytes 221192 | tf_op jit(solution)/shard_map/ppermute | solution.py:311
  32.9 4.9 %copy-start = (f32[1024]{0:T(1024)S(1)}, f32[1024]{0:T(1024)}, u32[]{:S(2)}) copy-start(f32[1024]{0:T(1024)} %param.15) | copy-start | bytes 12292

commit v2 on v1

--- a/solution.py
+++ b/solution.py
@@ -83,7 +83,7 @@
         out[entries + segments : entries + segments + 1, :] = mine[slots - 1 :]
 
 
-def slot_places(dest, me, members):
+def slot_places(dest, me, members, planes):
     slots = dest.shape[1]
     a, b = iota((slots, slots), 0), iota((slots, slots), 1)
     column = jnp.sum(jnp.where(a == b, dest.astype(jnp.float32), 0.0), axis=1, keepdims=True)
@@ -91,7 +91,8 @@
     owner = column // TB_DEV
     earlier = ones_of((owner == dest // TB_DEV) & (b < a))
     rank = jnp.sum(earlier, axis=1, keepdims=True).astype(jnp.int32)
-    return owner & (members - 1), (owner // members) ^ (me // members), rank, column & (TB_DEV - 1)
+    plane = (owner // members - me // members + 1) & (planes - 1)
+    return owner & (members - 1), plane, rank, column & (TB_DEV - 1)
 
 
 def run_segments(tiles, slots, meta, x, w, acc):
@@ -168,7 +169,7 @@
     block = jnp.where(inner, place - rim, jnp.where(at_hand, own + offset, offset))
     tile_ids = iota((1, tiles), 1)
     alive = tile_ids < live
-    member, plane, rank, block_row = slot_places(dests[...], me, members)
+    member, plane, rank, block_row = slot_places(dests[...], me, members, spans[-1][1])
     member = member ^ (me & (members - 1))
     kinds = [alive & at_hand & (tile_ids < tiles // 2), alive & at_hand & (tile_ids >= tiles // 2)]
     kinds += [alive & ~at_hand]
@@ -249,7 +250,7 @@
                 sums = [s + jnp.where(mark == k, value, 0.0) for k, s in enumerate(sums)]
         for k, s in enumerate(sums):
             if len(outs) == 1:
-                outs[0][(me[0] ^ m) * TB_DEV + k] = s.astype(outs[0].dtype)
+                outs[0][((me[0] + m - 1) & (planes - 1)) * TB_DEV + k] = s.astype(outs[0].dtype)
             else:
                 outs[m][k] = s.astype(outs[m].dtype)
 
@@ -309,6 +310,9 @@
 
     def swap(x, q):
         return lax.ppermute(x, "dom", [(i, i ^ q) for i in range(peers)])
+
+    def shift(x, m):
+        return lax.ppermute(x, "dom", [(i, (i + m * members) % peers) for i in range(peers)])
 
     near = swap(source, 1)
     far = lax.ppermute(
@@ -399,7 +403,7 @@
     for (lo, hi), (own, rows) in zip(spans, own_rows):
         if by_swap:
             part_shapes = [
-                jax.ShapeDtypeStruct(part, jnp.bfloat16) if m else pltpu.VMEM(part, jnp.float32)
+                pltpu.VMEM(part, jnp.float32) if m == 1 else jax.ShapeDtypeStruct(part, jnp.bfloat16)
                 for m in range(lo, hi)
             ]
         else:
@@ -413,7 +417,7 @@
             name="plane_sum",
         )((me // members)[None], in_vmem(own), *rows)
         if by_swap:
-            parts += [swap(s, m * members) if m else s for m, s in zip(range(lo, hi), sums)]
+            parts += [s if m == 1 else shift(s, m - 1) for m, s in zip(range(lo, hi), sums)][::-1]
         else:
             columns = [[z * members + i for z in range(planes)] for i in range(members)]
             parts.append(lax.all_to_all(sums[0], "dom", 0, 0, tiled=True, axis_index_groups=columns))

time: 39.2 us -> 38.6 us (0.985)
  waiting for transfers between devices: 8.29 us -> 6.16 us
  starting transfers between devices: 19 us -> 20.3 us
    ppermute x0 -> x3, starting transfers between devices: none -> 6.69 us  [shift(): lax.ppermute(x, 'dom', [(i, (i + m * members) % peers) for i in range(pee...]
    ppermute x10 -> x7, starting transfers between devices: 13.2 us -> 7.85 us  [swap(): return lax.ppermute(x, 'dom', [(i, i ^ q) for i in range(peers)])]
    ppermute x10 -> x7, waiting for transfers between devices: 6.11 us -> 2.59 us  [swap(): return lax.ppermute(x, 'dom', [(i, i ^ q) for i in range(peers)])]
    ppermute x0 -> x3, waiting for transfers between devices: none -> 1.4 us  [shift(): lax.ppermute(x, 'dom', [(i, (i + m * members) % peers) for i in range(pee...]
  transfers between devices with their start and end apart: 11 -> 11, of which waited for: 4 -> 5; matrix products, arithmetic and copies ran while one was open for 6% -> 7% of each run, Pallas kernels for 13% -> 13%
where the time goes in v2:
time: 38.6 us; the launch traced here: 38.2 us
  starting transfers between devices  20.3 us (53%)
  Pallas kernels  7.95 us (21%)
  waiting for transfers between devices  6.16 us (16%)
  local copies, waits for them, and re-layouts  2.41 us (6%)
  between operations  1.37 us (4%)
    ppermute x7, starting transfers between devices, swap(): return lax.ppermute(x, 'dom', [(i, i ^ q) for i in range(peers)])  7.85 us
    ppermute x3, starting transfers between devices, shift(): lax.ppermute(x, 'dom', [(i, (i + m * members) % peers) for i in range(pee...  6.69 us
    ppermute x1, starting transfers between devices, local(): lax.ppermute(lax.dynamic_slice_in_dim(source, core * width, width, axis=1...  5.73 us
    pallas_call x1, Pallas kernels, local(): pl.pallas_call(functools.partial(early_kernel, members, spans), out_shape...  4.84 us
    ppermute x7, waiting for transfers between devices, swap(): return lax.ppermute(x, 'dom', [(i, i ^ q) for i in range(peers)])  2.59 us
    ppermute x1, waiting for transfers between devices, local(): lax.ppermute(lax.dynamic_slice_in_dim(source, core * width, width, axis=1...  2.17 us
    pallas_call x1, Pallas kernels, local(): pl.pallas_call(functools.partial(late_kernel, tiles, slots, members), out...  1.51 us
    ppermute x3, waiting for transfers between devices, shift(): lax.ppermute(x, 'dom', [(i, (i + m * members) % peers) for i in range(pee...  1.4 us
  transfers between devices with their start and end apart: 11, of which 5 were waited for; matrix products, arithmetic and copies ran while one was open for 7% of the time, Pallas kernels for 13%

profile of v2, /device:TPU:0, one launch (start us, length us, event | category | flops | bytes accessed | tf_op | source)
XLA Modules:
  0.0 38.2 jit_solution(2524634654370919510)
XLA Ops:
  0.6 0.5 %collective-permute-start = (bf16[72,8192]{1,0:T(8,128)(2,1)}, bf16[72,8192]{1,0:T(8,128)(2,1)S(1)}, u32[]{:S(2)}, u32[]{:S(2)}) collective-permute-start(bf16[72,8192]{1,0:T(8,128)(2,1)} %refs_3_.1), channel_id=1, source_target_pairs={{0,1},{1,0},{2,3},{3,2},{4,5},{5,4},{6,7},{7,6},{8,9},{9,8},{10,11... | collective-permute-start | bytes 3538952 | tf_op jit(solution)/shard_map/ppermute | solution.py:312
  1.1 1.1 %constant_dynamic-slice_fusion = bf16[72,4096]{1,0:T(8,128)(2,1)S(1)} fusion(bf16[72,8192]{1,0:T(8,128)(2,1)} %refs_3_.1, s32[]{:T(128)S(6)} %select_n.48), kind=kLoop, calls=%fused_computation.19 | loop fusion | bytes 1179652 | tf_op jit(solution)/shard_map/dynamic_slice | solution.py:319
  2.3 5.7 %collective-permute-start.1 = (bf16[72,4096]{1,0:T(8,128)(2,1)S(1)}, bf16[72,4096]{1,0:T(8,128)(2,1)S(1)}, u32[]{:S(2)}, u32[]{:S(2)}) collective-permute-start(bf16[72,4096]{1,0:T(8,128)(2,1)S(1)} %constant_dynamic-slice_fusion), channel_id=1, source_target_pairs={{0,15},{1,2},{2,1},{3,4},{4,3},{5,6},{6,5},{7,8},{8,7},{9,10},{10,... | collective-permute-start | bytes 1769480 | tf_op jit(solution)/shard_map/ppermute | solution.py:318
  8.6 0.0 collective-permute-done.refs_4_
  8.6 4.8 %early_tiles.1 = (f32[16,72,128]{2,1,0:T(8,128)S(1)}, bf16[513,128,128]{2,1,0:T(8,128)(2,1)S(1)}, s32[16,128]{1,0:T(8,128)S(1)}, bf16[3,16,128]{2,1,0:T(8,128)(2,1)S(1)}, bf16[3,16,128]{2,1,0:T(8,128)(2,1)S(1)}) custom-call(s32[1]{0:T(128)} %bitcast.4.me, s32[1]{0:T(128)S(6)} %copy.13.count, s32[1,512]{1,0:T(1,128)} %bitcast.13, s32[1,512]{1,0:T(1,128)} %bitcast.14, ...), custom_call_target="tpu_custom_call" | custom-call | flops 1207959552 | bytes 16777216 | tf_op jit(solution)/shard_map/early_tiles/pallas_call | solution.py:338
  13.5 2.2 %collective-permute-done.1.far = bf16[72,4096]{1,0:T(8,128)(2,1)S(1)} collective-permute-done((bf16[72,4096]{1,0:T(8,128)(2,1)S(1)}, bf16[72,4096]{1,0:T(8,128)(2,1)S(1)}, u32[]{:S(2)}, u32[]{:S(2)}) %collective-permute-start.1) | collective-permute-done | bytes 589856 | tf_op jit(solution)/shard_map/ppermute | solution.py:318
  15.7 1.5 %late_tiles.1 = (f32[8,72,128]{2,1,0:T(8,128)S(1)}, bf16[304,128]{1,0:T(8,128)(2,1)S(1)}, bf16[304,128]{1,0:T(8,128)(2,1)S(1)}, bf16[304,128]{1,0:T(8,128)(2,1)S...) custom-call(s32[16,128]{1,0:T(8,128)S(1)} %get-tuple-element.19.meta, ...), custom_call_target="tpu_custom_call" | custom-call | flops 603979776 | bytes 589824 | tf_op jit(solution)/shard_map/late_tiles/pallas_call | solution.py:384
  17.2 4.9 %collective-permute-start.6 = (bf16[304,128]{1,0:T(8,128)(2,1)S(1)}, bf16[304,128]{1,0:T(8,128)(2,1)S(1)}, u32[]{:S(2)}, u32[]{:S(2)}) collective-permute-start(bf16[304,128]{1,0:T(8,128)(2,1)S(1)} %get-tuple-element.31), channel_id=1, source_target_pairs={{0,2},{1,3},{2,0},{3,1},{4,6},{5,7},{6,4},{7,5},{8,10},{9,11},{10,... | collective-permute-start | bytes 233480 | tf_op jit(solution)/shard_map/ppermute | solution.py:312
  22.1 0.5 %collective-permute-start.7 = (bf16[304,128]{1,0:T(8,128)(2,1)S(1)}, bf16[304,128]{1,0:T(8,128)(2,1)S(1)}, u32[]{:S(2)}, u32[]{:S(2)}) collective-permute-start(bf16[304,128]{1,0:T(8,128)(2,1)S(1)} %get-tuple-element.32), channel_id=1, source_target_pairs={{0,3},{1,2},{2,1},{3,0},{4,7},{5,6},{6,5},{7,4},{8,11},{9,10},{10,... | collective-permute-start | bytes 233480 | tf_op jit(solution)/shard_map/ppermute | solution.py:312
  22.5 0.0 collective-permute-start.8
  22.5 1.7 %collective-permute-start.2 = (bf16[304,128]{1,0:T(8,128)(2,1)S(1)}, bf16[304,128]{1,0:T(8,128)(2,1)S(1)}, u32[]{:S(2)}, u32[]{:S(2)}) collective-permute-start(bf16[304,128]{1,0:T(8,128)(2,1)S(1)} %get-tuple-element.25), channel_id=1, source_target_pairs={{0,2},{1,3},{2,0},{3,1},{4,6},{5,7},{6,4},{7,5},{8,10},{9,11},{10,... | collective-permute-start | bytes 233480 | tf_op jit(solution)/shard_map/ppermute | solution.py:312
  24.2 0.2 collective-permute-start.3
  24.4 0.7 %collective-permute-done.6.refs_0_ = bf16[304,128]{1,0:T(8,128)(2,1)S(1)} collective-permute-done((bf16[304,128]{1,0:T(8,128)(2,1)S(1)}, bf16[304,128]{1,0:T(8,128)(2,1)S(1)}, u32[]{:S(2)}, u32[]{:S(2)}) %collective-permute-start.6) | collective-permute-done | bytes 77856 | tf_op jit(solution)/shard_map/ppermute | solution.py:312
  25.1 0.1 collective-permute-start.4
  25.3 1.8 %collective-permute-done.7.refs_1_ = bf16[304,128]{1,0:T(8,128)(2,1)S(1)} collective-permute-done((bf16[304,128]{1,0:T(8,128)(2,1)S(1)}, bf16[304,128]{1,0:T(8,128)(2,1)S(1)}, u32[]{:S(2)}, u32[]{:S(2)}) %collective-permute-start.7) | collective-permute-done | bytes 77856 | tf_op jit(solution)/shard_map/ppermute | solution.py:312
  27.1 0.0 collective-permute-done.8.refs_2_
  27.1 0.1 plane_sum.3
  27.3 1.9 %collective-permute-start.10 = (bf16[4,72,128]{2,1,0:T(8,128)(2,1)S(1)}, bf16[4,72,128]{2,1,0:T(8,128)(2,1)S(1)}, u32[]{:S(2)}, u32[]{:S(2)}) collective-permute-start(bf16[4,72,128]{2,1,0:T(8,128)(2,1)S(1)} %get-tuple-element.35), channel_id=1, source_target_pairs={{0,4},{1,5},{2,6},{3,7},{4,8},{5,9},{6,10},{7,11},{8,12},{9,13},{1... | collective-permute-start | bytes 221192 | tf_op jit(solution)/shard_map/ppermute | solution.py:315
  29.2 2.6 %collective-permute-start.9 = (bf16[4,72,128]{2,1,0:T(8,128)(2,1)S(1)}, bf16[4,72,128]{2,1,0:T(8,128)(2,1)S(1)}, u32[]{:S(2)}, u32[]{:S(2)}) collective-permute-start(bf16[4,72,128]{2,1,0:T(8,128)(2,1)S(1)} %get-tuple-element.34), channel_id=1, source_target_pairs={{0,8},{1,9},{2,10},{3,11},{4,12},{5,13},{6,14},{7,15},{8,0},{9,1},... | collective-permute-start | bytes 221192 | tf_op jit(solution)/shard_map/ppermute | solution.py:315
  31.8 0.0 collective-permute-done.2.refs_0_
  31.8 0.0 collective-permute-done.3.refs_1_
  31.8 0.0 collective-permute-done.4.refs_2_
  31.8 0.1 plane_sum.2
  32.0 2.2 %collective-permute-start.5 = (bf16[4,72,128]{2,1,0:T(8,128)(2,1)S(1)}, bf16[4,72,128]{2,1,0:T(8,128)(2,1)S(1)}, u32[]{:S(2)}, u32[]{:S(2)}) collective-permute-start(bf16[4,72,128]{2,1,0:T(8,128)(2,1)S(1)} %get-tuple-element.29), channel_id=1, source_target_pairs={{0,12},{1,13},{2,14},{3,15},{4,0},{5,1},{6,2},{7,3},{8,4},{9,5},{1... | collective-permute-start | bytes 221192 | tf_op jit(solution)/shard_map/ppermute | solution.py:315
  34.1 0.1 fusion.choose
  34.2 0.0 copy-done.1
  34.2 0.0 copy-start
  34.2 1.3 %copy.12 = bf16[72,16,1024]{2,0,1:T(8,128)(2,1)S(1)} copy(bf16[72,16,1024]{2,1,0:T(8,128)(2,1)S(1)} %bitcast.12) | data formatting | bytes 4718592 | tf_op jit(solution)/shard_map/reshape | solution.py:375
  35.5 0.0 collective-permute-done.10.refs_3_
  35.5 1.3 %collective-permute-done.9.refs_2_ = bf16[4,72,128]{2,1,0:T(8,128)(2,1)S(1)} collective-permute-done((bf16[4,72,128]{2,1,0:T(8,128)(2,1)S(1)}, bf16[4,72,128]{2,1,0:T(8,128)(2,1)S(1)}, u32[]{:S(2)}, u32[]{:S(2)}) %collective-permute-start.9) | collective-permute-done | bytes 73760 | tf_op jit(solution)/shard_map/ppermute | solution.py:315
  36.9 0.1 collective-permute-done.5.refs_1_
  36.9 1.3 %embed.1 = (bf16[4,72,128]{2,1,0:T(8,128)(2,1)}, bf16[32,1024]{1,0:T(8,128)(2,1)}) custom-call(bf16[128,128]{1,0:T(8,128)(2,1)S(1)} %fusion.choose, bf16[16,72,1024]{2,1,0:T(8,128)(2,1)S(1)} %bitcast.10, f32[1,1024]{1,0:T(1,128)S(1)} %bitcast.11, f32[4,72,128]{2,1,0:T(8,128)S(1)} %get-tuple-element.28.refs_0_, ...), custom_call_target="tpu_custom_call" | custom-call | tf_op jit(solution)/shard_map/embed/pallas_call | solution.py:426
  (3 shorter events, 0.0 us)
Async XLA Ops:
  0.6 8.0 %collective-permute-start = (bf16[72,8192]{1,0:T(8,128)(2,1)}, bf16[72,8192]{1,0:T(8,128)(2,1)S(1)}, u32[]{:S(2)}, u32[]{:S(2)}) collective-permute-start(bf16[72,8192]{1,0:T(8,128)(2,1)} %refs_3_.1), channel_id=1, source_target_pairs={{0,1},{1,0},{2,3},{3,2},{4,5},{5,4},{6,7},{7,6},{8,9},{9,8},{10,11... | collective-permute-start | bytes 3538952 | tf_op jit(solution)/shard_map/ppermute | solution.py:312
  2.3 13.4 %collective-permute-start.1 = (bf16[72,4096]{1,0:T(8,128)(2,1)S(1)}, bf16[72,4096]{1,0:T(8,128)(2,1)S(1)}, u32[]{:S(2)}, u32[]{:S(2)}) collective-permute-start(bf16[72,4096]{1,0:T(8,128)(2,1)S(1)} %constant_dynamic-slice_fusion), channel_id=1, source_target_pairs={{0,15},{1,2},{2,1},{3,4},{4,3},{5,6},{6,5},{7,8},{8,7},{9,10},{10,... | collective-permute-start | bytes 1769480 | tf_op jit(solution)/shard_map/ppermute | solution.py:318
  15.7 18.5 %copy-start.1 = (bf16[1152,1024]{1,0:T(8,128)(2,1)S(1)}, bf16[1152,1024]{1,0:T(8,128)(2,1)}, u32[]{:S(2)}) copy-start(bf16[1152,1024]{1,0:T(8,128)(2,1)} %param.14) | copy-start | bytes 7077892
  17.2 8.0 %collective-permute-start.6 = (bf16[304,128]{1,0:T(8,128)(2,1)S(1)}, bf16[304,128]{1,0:T(8,128)(2,1)S(1)}, u32[]{:S(2)}, u32[]{:S(2)}) collective-permute-start(bf16[304,128]{1,0:T(8,128)(2,1)S(1)} %get-tuple-element.31), channel_id=1, source_target_pairs={{0,2},{1,3},{2,0},{3,1},{4,6},{5,7},{6,4},{7,5},{8,10},{9,11},{10,... | collective-permute-start | bytes 233480 | tf_op jit(solution)/shard_map/ppermute | solution.py:312
  22.1 5.0 %collective-permute-start.7 = (bf16[304,128]{1,0:T(8,128)(2,1)S(1)}, bf16[304,128]{1,0:T(8,128)(2,1)S(1)}, u32[]{:S(2)}, u32[]{:S(2)}) collective-permute-start(bf16[304,128]{1,0:T(8,128)(2,1)S(1)} %get-tuple-element.32), channel_id=1, source_target_pairs={{0,3},{1,2},{2,1},{3,0},{4,7},{5,6},{6,5},{7,4},{8,11},{9,10},{10,... | collective-permute-start | bytes 233480 | tf_op jit(solution)/shard_map/ppermute | solution.py:312
  22.5 4.6 %collective-permute-start.8 = (bf16[304,128]{1,0:T(8,128)(2,1)S(1)}, bf16[304,128]{1,0:T(8,128)(2,1)S(1)}, u32[]{:S(2)}, u32[]{:S(2)}) collective-permute-start(bf16[304,128]{1,0:T(8,128)(2,1)S(1)} %get-tuple-element.33), channel_id=1, source_target_pairs={{0,1},{1,0},{2,3},{3,2},{4,5},{5,4},{6,7},{7,6},{8,9},{9,8},{10,11... | collective-permute-start | bytes 233480 | tf_op jit(solution)/shard_map/ppermute | solution.py:312
  22.5 9.3 %collective-permute-start.2 = (bf16[304,128]{1,0:T(8,128)(2,1)S(1)}, bf16[304,128]{1,0:T(8,128)(2,1)S(1)}, u32[]{:S(2)}, u32[]{:S(2)}) collective-permute-start(bf16[304,128]{1,0:T(8,128)(2,1)S(1)} %get-tuple-element.25), channel_id=1, source_target_pairs={{0,2},{1,3},{2,0},{3,1},{4,6},{5,7},{6,4},{7,5},{8,10},{9,11},{10,... | collective-permute-start | bytes 233480 | tf_op jit(solution)/shard_map/ppermute | solution.py:312
  24.2 7.6 %collective-permute-start.3 = (bf16[304,128]{1,0:T(8,128)(2,1)S(1)}, bf16[304,128]{1,0:T(8,128)(2,1)S(1)}, u32[]{:S(2)}, u32[]{:S(2)}) collective-permute-start(bf16[304,128]{1,0:T(8,128)(2,1)S(1)} %get-tuple-element.26), channel_id=1, source_target_pairs={{0,3},{1,2},{2,1},{3,0},{4,7},{5,6},{6,5},{7,4},{8,11},{9,10},{10,... | collective-permute-start | bytes 233480 | tf_op jit(solution)/shard_map/ppermute | solution.py:312
  25.1 6.7 %collective-permute-start.4 = (bf16[304,128]{1,0:T(8,128)(2,1)S(1)}, bf16[304,128]{1,0:T(8,128)(2,1)S(1)}, u32[]{:S(2)}, u32[]{:S(2)}) collective-permute-start(bf16[304,128]{1,0:T(8,128)(2,1)S(1)} %get-tuple-element.27), channel_id=1, source_target_pairs={{0,1},{1,0},{2,3},{3,2},{4,5},{5,4},{6,7},{7,6},{8,9},{9,8},{10,11... | collective-permute-start | bytes 233480 | tf_op jit(solution)/shard_map/ppermute | solution.py:312
  27.3 8.3 %collective-permute-start.10 = (bf16[4,72,128]{2,1,0:T(8,128)(2,1)S(1)}, bf16[4,72,128]{2,1,0:T(8,128)(2,1)S(1)}, u32[]{:S(2)}, u32[]{:S(2)}) collective-permute-start(bf16[4,72,128]{2,1,0:T(8,128)(2,1)S(1)} %get-tuple-element.35), channel_id=1, source_target_pairs={{0,4},{1,5},{2,6},{3,7},{4,8},{5,9},{6,10},{7,11},{8,12},{9,13},{1... | collective-permute-start | bytes 221192 | tf_op jit(solution)/shard_map/ppermute | solution.py:315
  29.2 7.7 %collective-permute-start.9 = (bf16[4,72,128]{2,1,0:T(8,128)(2,1)S(1)}, bf16[4,72,128]{2,1,0:T(8,128)(2,1)S(1)}, u32[]{:S(2)}, u32[]{:S(2)}) collective-permute-start(bf16[4,72,128]{2,1,0:T(8,128)(2,1)S(1)} %get-tuple-element.34), channel_id=1, source_target_pairs={{0,8},{1,9},{2,10},{3,11},{4,12},{5,13},{6,14},{7,15},{8,0},{9,1},... | collective-permute-start | bytes 221192 | tf_op jit(solution)/shard_map/ppermute | solution.py:315
  32.0 5.0 %collective-permute-start.5 = (bf16[4,72,128]{2,1,0:T(8,128)(2,1)S(1)}, bf16[4,72,128]{2,1,0:T(8,128)(2,1)S(1)}, u32[]{:S(2)}, u32[]{:S(2)}) collective-permute-start(bf16[4,72,128]{2,1,0:T(8,128)(2,1)S(1)} %get-tuple-element.29), channel_id=1, source_target_pairs={{0,12},{1,13},{2,14},{3,15},{4,0},{5,1},{6,2},{7,3},{8,4},{9,5},{1... | collective-permute-start | bytes 221192 | tf_op jit(solution)/shard_map/ppermute | solution.py:315
  34.2 2.7 %copy-start = (f32[1024]{0:T(1024)S(1)}, f32[1024]{0:T(1024)}, u32[]{:S(2)}) copy-start(f32[1024]{0:T(1024)} %param.15) | copy-start | bytes 12292

commit v3 on v2

--- a/solution.py
+++ b/solution.py
@@ -397,7 +397,7 @@
     for i in range(len(spans)):
         own, *rows = late[i * members : (i + 1) * members]
         swapped = [swap(r, q + 1) for q, r in enumerate(rows)]
-        own_rows.append((own, swapped[1:] + swapped[:1]))
+        own_rows.append((own, swapped[::-1]))
 
     parts = []
     for (lo, hi), (own, rows) in zip(spans, own_rows):

time: 38.6 us -> 38.7 us (level); the launches traced: 38.2 us -> 38.9 us
  Pallas kernels: 7.95 us -> 14.5 us
  starting transfers between devices: 20.3 us -> 17 us
  waiting for transfers between devices: 6.16 us -> 3.56 us
    pallas_call x1, Pallas kernels: 4.84 us -> 10.7 us  [local(): pl.pallas_call(functools.partial(early_kernel, members, spans), out_shape...]
    ppermute x7, starting transfers between devices: 7.85 us -> 4.06 us  [swap(): return lax.ppermute(x, 'dom', [(i, i ^ q) for i in range(peers)])]
    ppermute x1, waiting for transfers between devices: 2.17 us -> 0.01 us  [local(): lax.ppermute(lax.dynamic_slice_in_dim(source, core * width, width, axis=1...]
    ppermute x7, waiting for transfers between devices: 2.59 us -> 1.78 us  [swap(): return lax.ppermute(x, 'dom', [(i, i ^ q) for i in range(peers)])]
    pallas_call x1, Pallas kernels: 1.51 us -> 2.23 us  [local(): pl.pallas_call(functools.partial(late_kernel, tiles, slots, members), out...]
    ppermute x3, starting transfers between devices: 6.69 us -> 7.18 us  [shift(): lax.ppermute(x, 'dom', [(i, (i + m * members) % peers) for i in range(pee...]
  transfers between devices with their start and end apart: 11 -> 11, of which waited for: 5 -> 4; matrix products, arithmetic and copies ran while one was open for 7% -> 6% of each run, Pallas kernels for 13% -> 28%
where the time goes in v3:
time: 38.7 us; the launch traced here: 38.9 us
  starting transfers between devices  17 us (44%)
  Pallas kernels  14.5 us (37%)
  waiting for transfers between devices  3.56 us (9%)
  local copies, waits for them, and re-layouts  2.41 us (6%)
  between operations  1.4 us (4%)
    pallas_call x1, Pallas kernels, local(): pl.pallas_call(functools.partial(early_kernel, members, spans), out_shape...  10.7 us
    ppermute x3, starting transfers between devices, shift(): lax.ppermute(x, 'dom', [(i, (i + m * members) % peers) for i in range(pee...  7.18 us
    ppermute x1, starting transfers between devices, local(): lax.ppermute(lax.dynamic_slice_in_dim(source, core * width, width, axis=1...  5.73 us
    ppermute x7, starting transfers between devices, swap(): return lax.ppermute(x, 'dom', [(i, i ^ q) for i in range(peers)])  4.06 us
    pallas_call x1, Pallas kernels, local(): pl.pallas_call(functools.partial(late_kernel, tiles, slots, members), out...  2.23 us
    ppermute x3, waiting for transfers between devices, shift(): lax.ppermute(x, 'dom', [(i, (i + m * members) % peers) for i in range(pee...  1.78 us
    ppermute x7, waiting for transfers between devices, swap(): return lax.ppermute(x, 'dom', [(i, i ^ q) for i in range(peers)])  1.78 us
    pallas_call x1, Pallas kernels, local(): pl.pallas_call(final_kernel, out_shape=(jax.ShapeDtypeStruct(part, jnp.bf...  1.3 us
  transfers between devices with their start and end apart: 11, of which 4 were waited for; matrix products, arithmetic and copies ran while one was open for 6% of the time, Pallas kernels for 28%

profile of v3, /device:TPU:0, one launch (start us, length us, event | category | flops | bytes accessed | tf_op | source)
XLA Modules:
  0.0 38.9 jit_solution(7215719745680173640)
XLA Ops:
  0.6 0.5 %collective-permute-start = (bf16[72,8192]{1,0:T(8,128)(2,1)}, bf16[72,8192]{1,0:T(8,128)(2,1)S(1)}, u32[]{:S(2)}, u32[]{:S(2)}) collective-permute-start(bf16[72,8192]{1,0:T(8,128)(2,1)} %refs_3_.1), channel_id=1, source_target_pairs={{0,1},{1,0},{2,3},{3,2},{4,5},{5,4},{6,7},{7,6},{8,9},{9,8},{10,11... | collective-permute-start | bytes 3538952 | tf_op jit(solution)/shard_map/ppermute | solution.py:312
  1.1 1.1 %constant_dynamic-slice_fusion = bf16[72,4096]{1,0:T(8,128)(2,1)S(1)} fusion(bf16[72,8192]{1,0:T(8,128)(2,1)} %refs_3_.1, s32[]{:T(128)S(6)} %select_n.48), kind=kLoop, calls=%fused_computation.19 | loop fusion | bytes 1179652 | tf_op jit(solution)/shard_map/dynamic_slice | solution.py:319
  2.3 5.7 %collective-permute-start.1 = (bf16[72,4096]{1,0:T(8,128)(2,1)S(1)}, bf16[72,4096]{1,0:T(8,128)(2,1)S(1)}, u32[]{:S(2)}, u32[]{:S(2)}) collective-permute-start(bf16[72,4096]{1,0:T(8,128)(2,1)S(1)} %constant_dynamic-slice_fusion), channel_id=1, source_target_pairs={{0,15},{1,2},{2,1},{3,4},{4,3},{5,6},{6,5},{7,8},{8,7},{9,10},{10,... | collective-permute-start | bytes 1769480 | tf_op jit(solution)/shard_map/ppermute | solution.py:318
  8.6 0.0 collective-permute-done.refs_4_
  8.6 10.7 %early_tiles.1 = (f32[16,72,128]{2,1,0:T(8,128)S(1)}, bf16[513,128,128]{2,1,0:T(8,128)(2,1)S(1)}, s32[16,128]{1,0:T(8,128)S(1)}, bf16[3,16,128]{2,1,0:T(8,128)(2,1)S(1)}, bf16[3,16,128]{2,1,0:T(8,128)(2,1)S(1)}) custom-call(s32[1]{0:T(128)} %bitcast.4.me, s32[1]{0:T(128)S(6)} %copy.13.count, s32[1,512]{1,0:T(1,128)} %bitcast.13, s32[1,512]{1,0:T(1,128)} %bitcast.14, ...), custom_call_target="tpu_custom_call" | custom-call | flops 1207959552 | bytes 16777216 | tf_op jit(solution)/shard_map/early_tiles/pallas_call | solution.py:338
  19.3 0.0 collective-permute-done.1.far
  19.3 0.0 copy-start.1
  19.4 2.2 %late_tiles.1 = (f32[8,72,128]{2,1,0:T(8,128)S(1)}, bf16[304,128]{1,0:T(8,128)(2,1)S(1)}, bf16[304,128]{1,0:T(8,128)(2,1)S(1)}, bf16[304,128]{1,0:T(8,128)(2,1)S...) custom-call(s32[16,128]{1,0:T(8,128)S(1)} %get-tuple-element.19.meta, ...), custom_call_target="tpu_custom_call" | custom-call | flops 603979776 | bytes 589824 | tf_op jit(solution)/shard_map/late_tiles/pallas_call | solution.py:384
  21.6 0.1 collective-permute-start.6
  21.7 0.5 %collective-permute-start.7 = (bf16[304,128]{1,0:T(8,128)(2,1)S(1)}, bf16[304,128]{1,0:T(8,128)(2,1)S(1)}, u32[]{:S(2)}, u32[]{:S(2)}) collective-permute-start(bf16[304,128]{1,0:T(8,128)(2,1)S(1)} %get-tuple-element.32), channel_id=1, source_target_pairs={{0,2},{1,3},{2,0},{3,1},{4,6},{5,7},{6,4},{7,5},{8,10},{9,11},{10,... | collective-permute-start | bytes 233480 | tf_op jit(solution)/shard_map/ppermute | solution.py:312
  22.2 1.3 %collective-permute-start.8 = (bf16[304,128]{1,0:T(8,128)(2,1)S(1)}, bf16[304,128]{1,0:T(8,128)(2,1)S(1)}, u32[]{:S(2)}, u32[]{:S(2)}) collective-permute-start(bf16[304,128]{1,0:T(8,128)(2,1)S(1)} %get-tuple-element.33), channel_id=1, source_target_pairs={{0,1},{1,0},{2,3},{3,2},{4,5},{5,4},{6,7},{7,6},{8,9},{9,8},{10,11... | collective-permute-start | bytes 233480 | tf_op jit(solution)/shard_map/ppermute | solution.py:312
  23.5 0.4 collective-permute-start.2
  23.9 1.3 %collective-permute-start.3 = (bf16[304,128]{1,0:T(8,128)(2,1)S(1)}, bf16[304,128]{1,0:T(8,128)(2,1)S(1)}, u32[]{:S(2)}, u32[]{:S(2)}) collective-permute-start(bf16[304,128]{1,0:T(8,128)(2,1)S(1)} %get-tuple-element.26), channel_id=1, source_target_pairs={{0,2},{1,3},{2,0},{3,1},{4,6},{5,7},{6,4},{7,5},{8,10},{9,11},{10,... | collective-permute-start | bytes 233480 | tf_op jit(solution)/shard_map/ppermute | solution.py:312
  25.2 0.5 %collective-permute-done.6.refs_0_ = bf16[304,128]{1,0:T(8,128)(2,1)S(1)} collective-permute-done((bf16[304,128]{1,0:T(8,128)(2,1)S(1)}, bf16[304,128]{1,0:T(8,128)(2,1)S(1)}, u32[]{:S(2)}, u32[]{:S(2)}) %collective-permute-start.6) | collective-permute-done | bytes 77856 | tf_op jit(solution)/shard_map/ppermute | solution.py:312
  25.7 0.0 collective-permute-start.4
  25.7 1.2 %collective-permute-done.7.refs_1_ = bf16[304,128]{1,0:T(8,128)(2,1)S(1)} collective-permute-done((bf16[304,128]{1,0:T(8,128)(2,1)S(1)}, bf16[304,128]{1,0:T(8,128)(2,1)S(1)}, u32[]{:S(2)}, u32[]{:S(2)}) %collective-permute-start.7) | collective-permute-done | bytes 77856 | tf_op jit(solution)/shard_map/ppermute | solution.py:312
  26.9 0.0 collective-permute-done.8.refs_2_
  26.9 0.1 plane_sum.3
  27.1 2.5 %collective-permute-start.10 = (bf16[4,72,128]{2,1,0:T(8,128)(2,1)S(1)}, bf16[4,72,128]{2,1,0:T(8,128)(2,1)S(1)}, u32[]{:S(2)}, u32[]{:S(2)}) collective-permute-start(bf16[4,72,128]{2,1,0:T(8,128)(2,1)S(1)} %get-tuple-element.35), channel_id=1, source_target_pairs={{0,4},{1,5},{2,6},{3,7},{4,8},{5,9},{6,10},{7,11},{8,12},{9,13},{1... | collective-permute-start | bytes 221192 | tf_op jit(solution)/shard_map/ppermute | solution.py:315
  29.6 2.9 %collective-permute-start.9 = (bf16[4,72,128]{2,1,0:T(8,128)(2,1)S(1)}, bf16[4,72,128]{2,1,0:T(8,128)(2,1)S(1)}, u32[]{:S(2)}, u32[]{:S(2)}) collective-permute-start(bf16[4,72,128]{2,1,0:T(8,128)(2,1)S(1)} %get-tuple-element.34), channel_id=1, source_target_pairs={{0,8},{1,9},{2,10},{3,11},{4,12},{5,13},{6,14},{7,15},{8,0},{9,1},... | collective-permute-start | bytes 221192 | tf_op jit(solution)/shard_map/ppermute | solution.py:315
  32.5 0.0 collective-permute-done.2.refs_0_
  32.5 0.0 collective-permute-done.3.refs_1_
  32.5 0.0 collective-permute-done.4.refs_2_
  32.5 0.1 plane_sum.2
  32.7 1.8 %collective-permute-start.5 = (bf16[4,72,128]{2,1,0:T(8,128)(2,1)S(1)}, bf16[4,72,128]{2,1,0:T(8,128)(2,1)S(1)}, u32[]{:S(2)}, u32[]{:S(2)}) collective-permute-start(bf16[4,72,128]{2,1,0:T(8,128)(2,1)S(1)} %get-tuple-element.29), channel_id=1, source_target_pairs={{0,12},{1,13},{2,14},{3,15},{4,0},{5,1},{6,2},{7,3},{8,4},{9,5},{1... | collective-permute-start | bytes 221192 | tf_op jit(solution)/shard_map/ppermute | solution.py:315
  34.4 0.1 fusion.choose
  34.5 0.0 copy-start
  34.5 1.3 %copy.12 = bf16[72,16,1024]{2,0,1:T(8,128)(2,1)S(1)} copy(bf16[72,16,1024]{2,1,0:T(8,128)(2,1)S(1)} %bitcast.12) | data formatting | bytes 4718592 | tf_op jit(solution)/shard_map/reshape | solution.py:375
  35.8 0.0 collective-permute-done.10.refs_3_
  35.9 1.5 %collective-permute-done.9.refs_2_ = bf16[4,72,128]{2,1,0:T(8,128)(2,1)S(1)} collective-permute-done((bf16[4,72,128]{2,1,0:T(8,128)(2,1)S(1)}, bf16[4,72,128]{2,1,0:T(8,128)(2,1)S(1)}, u32[]{:S(2)}, u32[]{:S(2)}) %collective-permute-start.9) | collective-permute-done | bytes 73760 | tf_op jit(solution)/shard_map/ppermute | solution.py:315
  37.4 0.2 collective-permute-done.5.refs_1_
  37.6 1.3 %embed.1 = (bf16[4,72,128]{2,1,0:T(8,128)(2,1)}, bf16[32,1024]{1,0:T(8,128)(2,1)}) custom-call(bf16[128,128]{1,0:T(8,128)(2,1)S(1)} %fusion.choose, bf16[16,72,1024]{2,1,0:T(8,128)(2,1)S(1)} %bitcast.10, f32[1,1024]{1,0:T(1,128)S(1)} %bitcast.11, f32[4,72,128]{2,1,0:T(8,128)S(1)} %get-tuple-element.28.refs_0_, ...), custom_call_target="tpu_custom_call" | custom-call | tf_op jit(solution)/shard_map/embed/pallas_call | solution.py:426
  (3 shorter events, 0.0 us)
Async XLA Ops:
  0.6 8.0 %collective-permute-start = (bf16[72,8192]{1,0:T(8,128)(2,1)}, bf16[72,8192]{1,0:T(8,128)(2,1)S(1)}, u32[]{:S(2)}, u32[]{:S(2)}) collective-permute-start(bf16[72,8192]{1,0:T(8,128)(2,1)} %refs_3_.1), channel_id=1, source_target_pairs={{0,1},{1,0},{2,3},{3,2},{4,5},{5,4},{6,7},{7,6},{8,9},{9,8},{10,11... | collective-permute-start | bytes 3538952 | tf_op jit(solution)/shard_map/ppermute | solution.py:312
  2.3 17.1 %collective-permute-start.1 = (bf16[72,4096]{1,0:T(8,128)(2,1)S(1)}, bf16[72,4096]{1,0:T(8,128)(2,1)S(1)}, u32[]{:S(2)}, u32[]{:S(2)}) collective-permute-start(bf16[72,4096]{1,0:T(8,128)(2,1)S(1)} %constant_dynamic-slice_fusion), channel_id=1, source_target_pairs={{0,15},{1,2},{2,1},{3,4},{4,3},{5,6},{6,5},{7,8},{8,7},{9,10},{10,... | collective-permute-start | bytes 1769480 | tf_op jit(solution)/shard_map/ppermute | solution.py:318
  19.3 15.2 %copy-start.1 = (bf16[1152,1024]{1,0:T(8,128)(2,1)S(1)}, bf16[1152,1024]{1,0:T(8,128)(2,1)}, u32[]{:S(2)}) copy-start(bf16[1152,1024]{1,0:T(8,128)(2,1)} %param.14) | copy-start | bytes 7077892
  21.6 4.1 %collective-permute-start.6 = (bf16[304,128]{1,0:T(8,128)(2,1)S(1)}, bf16[304,128]{1,0:T(8,128)(2,1)S(1)}, u32[]{:S(2)}, u32[]{:S(2)}) collective-permute-start(bf16[304,128]{1,0:T(8,128)(2,1)S(1)} %get-tuple-element.31), channel_id=1, source_target_pairs={{0,3},{1,2},{2,1},{3,0},{4,7},{5,6},{6,5},{7,4},{8,11},{9,10},{10,... | collective-permute-start | bytes 233480 | tf_op jit(solution)/shard_map/ppermute | solution.py:312
  21.7 5.2 %collective-permute-start.7 = (bf16[304,128]{1,0:T(8,128)(2,1)S(1)}, bf16[304,128]{1,0:T(8,128)(2,1)S(1)}, u32[]{:S(2)}, u32[]{:S(2)}) collective-permute-start(bf16[304,128]{1,0:T(8,128)(2,1)S(1)} %get-tuple-element.32), channel_id=1, source_target_pairs={{0,2},{1,3},{2,0},{3,1},{4,6},{5,7},{6,4},{7,5},{8,10},{9,11},{10,... | collective-permute-start | bytes 233480 | tf_op jit(solution)/shard_map/ppermute | solution.py:312
  22.2 4.8 %collective-permute-start.8 = (bf16[304,128]{1,0:T(8,128)(2,1)S(1)}, bf16[304,128]{1,0:T(8,128)(2,1)S(1)}, u32[]{:S(2)}, u32[]{:S(2)}) collective-permute-start(bf16[304,128]{1,0:T(8,128)(2,1)S(1)} %get-tuple-element.33), channel_id=1, source_target_pairs={{0,1},{1,0},{2,3},{3,2},{4,5},{5,4},{6,7},{7,6},{8,9},{9,8},{10,11... | collective-permute-start | bytes 233480 | tf_op jit(solution)/shard_map/ppermute | solution.py:312
  23.5 9.0 %collective-permute-start.2 = (bf16[304,128]{1,0:T(8,128)(2,1)S(1)}, bf16[304,128]{1,0:T(8,128)(2,1)S(1)}, u32[]{:S(2)}, u32[]{:S(2)}) collective-permute-start(bf16[304,128]{1,0:T(8,128)(2,1)S(1)} %get-tuple-element.25), channel_id=1, source_target_pairs={{0,3},{1,2},{2,1},{3,0},{4,7},{5,6},{6,5},{7,4},{8,11},{9,10},{10,... | collective-permute-start | bytes 233480 | tf_op jit(solution)/shard_map/ppermute | solution.py:312
  23.9 8.6 %collective-permute-start.3 = (bf16[304,128]{1,0:T(8,128)(2,1)S(1)}, bf16[304,128]{1,0:T(8,128)(2,1)S(1)}, u32[]{:S(2)}, u32[]{:S(2)}) collective-permute-start(bf16[304,128]{1,0:T(8,128)(2,1)S(1)} %get-tuple-element.26), channel_id=1, source_target_pairs={{0,2},{1,3},{2,0},{3,1},{4,6},{5,7},{6,4},{7,5},{8,10},{9,11},{10,... | collective-permute-start | bytes 233480 | tf_op jit(solution)/shard_map/ppermute | solution.py:312
  25.7 6.8 %collective-permute-start.4 = (bf16[304,128]{1,0:T(8,128)(2,1)S(1)}, bf16[304,128]{1,0:T(8,128)(2,1)S(1)}, u32[]{:S(2)}, u32[]{:S(2)}) collective-permute-start(bf16[304,128]{1,0:T(8,128)(2,1)S(1)} %get-tuple-element.27), channel_id=1, source_target_pairs={{0,1},{1,0},{2,3},{3,2},{4,5},{5,4},{6,7},{7,6},{8,9},{9,8},{10,11... | collective-permute-start | bytes 233480 | tf_op jit(solution)/shard_map/ppermute | solution.py:312
  27.1 8.8 %collective-permute-start.10 = (bf16[4,72,128]{2,1,0:T(8,128)(2,1)S(1)}, bf16[4,72,128]{2,1,0:T(8,128)(2,1)S(1)}, u32[]{:S(2)}, u32[]{:S(2)}) collective-permute-start(bf16[4,72,128]{2,1,0:T(8,128)(2,1)S(1)} %get-tuple-element.35), channel_id=1, source_target_pairs={{0,4},{1,5},{2,6},{3,7},{4,8},{5,9},{6,10},{7,11},{8,12},{9,13},{1... | collective-permute-start | bytes 221192 | tf_op jit(solution)/shard_map/ppermute | solution.py:315
  29.6 7.8 %collective-permute-start.9 = (bf16[4,72,128]{2,1,0:T(8,128)(2,1)S(1)}, bf16[4,72,128]{2,1,0:T(8,128)(2,1)S(1)}, u32[]{:S(2)}, u32[]{:S(2)}) collective-permute-start(bf16[4,72,128]{2,1,0:T(8,128)(2,1)S(1)} %get-tuple-element.34), channel_id=1, source_target_pairs={{0,8},{1,9},{2,10},{3,11},{4,12},{5,13},{6,14},{7,15},{8,0},{9,1},... | collective-permute-start | bytes 221192 | tf_op jit(solution)/shard_map/ppermute | solution.py:315
  32.7 5.0 %collective-permute-start.5 = (bf16[4,72,128]{2,1,0:T(8,128)(2,1)S(1)}, bf16[4,72,128]{2,1,0:T(8,128)(2,1)S(1)}, u32[]{:S(2)}, u32[]{:S(2)}) collective-permute-start(bf16[4,72,128]{2,1,0:T(8,128)(2,1)S(1)} %get-tuple-element.29), channel_id=1, source_target_pairs={{0,12},{1,13},{2,14},{3,15},{4,0},{5,1},{6,2},{7,3},{8,4},{9,5},{1... | collective-permute-start | bytes 221192 | tf_op jit(solution)/shard_map/ppermute | solution.py:315
  34.5 3.1 %copy-start = (f32[1024]{0:T(1024)S(1)}, f32[1024]{0:T(1024)}, u32[]{:S(2)}) copy-start(f32[1024]{0:T(1024)} %param.15) | copy-start | bytes 12292

commit v4 on v2

--- a/solution.py
+++ b/solution.py
@@ -212,8 +212,8 @@
     n = (len(rest) - 1) // (members + 1)
     labels, outs, acc = rest[:n], rest[n:-1], rest[-1]
     acc[:slots] = partial[...]
+    run_segments(tiles, slots, meta, far, held, acc)
     acc[slots] = jnp.zeros(acc.shape[1:], acc.dtype)
-    run_segments(tiles, slots, meta, far, held, acc)
     spot = sum(list_rows(tiles, slots)) + 1
     p = 0
 

time: 38.6 us -> 39.1 us (1.013)
  Pallas kernels: 7.95 us -> 14.5 us
  starting transfers between devices: 20.3 us -> 16.7 us
  waiting for transfers between devices: 6.16 us -> 4.04 us
    pallas_call x1, Pallas kernels: 4.84 us -> 10.6 us  [local(): pl.pallas_call(functools.partial(early_kernel, members, spans), out_shape...]
    ppermute x7, starting transfers between devices: 7.85 us -> 4.08 us  [swap(): return lax.ppermute(x, 'dom', [(i, i ^ q) for i in range(peers)])]
    ppermute x1, waiting for transfers between devices: 2.17 us -> 0.01 us  [local(): lax.ppermute(lax.dynamic_slice_in_dim(source, core * width, width, axis=1...]
    ppermute x3, waiting for transfers between devices: 1.4 us -> 2.29 us  [shift(): lax.ppermute(x, 'dom', [(i, (i + m * members) % peers) for i in range(pee...]
    ppermute x7, waiting for transfers between devices: 2.59 us -> 1.75 us  [swap(): return lax.ppermute(x, 'dom', [(i, i ^ q) for i in range(peers)])]
    pallas_call x1, Pallas kernels: 1.51 us -> 2.22 us  [local(): pl.pallas_call(functools.partial(late_kernel, tiles, slots, members), out...]
  transfers between devices with their start and end apart: 11 -> 11, of which waited for: 5 -> 3; matrix products, arithmetic and copies ran while one was open for 7% -> 6% of each run, Pallas kernels for 13% -> 28%
where the time goes in v4:
time: 39.1 us
  starting transfers between devices  16.7 us (43%)
  Pallas kernels  14.5 us (37%)
  waiting for transfers between devices  4.04 us (10%)
  local copies, waits for them, and re-layouts  2.41 us (6%)
  between operations  1.39 us (4%)
    pallas_call x1, Pallas kernels, local(): pl.pallas_call(functools.partial(early_kernel, members, spans), out_shape...  10.6 us
    ppermute x3, starting transfers between devices, shift(): lax.ppermute(x, 'dom', [(i, (i + m * members) % peers) for i in range(pee...  6.92 us
    ppermute x1, starting transfers between devices, local(): lax.ppermute(lax.dynamic_slice_in_dim(source, core * width, width, axis=1...  5.73 us
    ppermute x7, starting transfers between devices, swap(): return lax.ppermute(x, 'dom', [(i, i ^ q) for i in range(peers)])  4.08 us
    ppermute x3, waiting for transfers between devices, shift(): lax.ppermute(x, 'dom', [(i, (i + m * members) % peers) for i in range(pee...  2.29 us
    pallas_call x1, Pallas kernels, local(): pl.pallas_call(functools.partial(late_kernel, tiles, slots, members), out...  2.22 us
    ppermute x7, waiting for transfers between devices, swap(): return lax.ppermute(x, 'dom', [(i, i ^ q) for i in range(peers)])  1.75 us
    pallas_call x1, Pallas kernels, local(): pl.pallas_call(final_kernel, out_shape=(jax.ShapeDtypeStruct(part, jnp.bf...  1.3 us
  transfers between devices with their start and end apart: 11, of which 3 were waited for; matrix products, arithmetic and copies ran while one was open for 6% of the time, Pallas kernels for 28%

profile of v4, /device:TPU:0, one launch (start us, length us, event | category | flops | bytes accessed | tf_op | source)
XLA Modules:
  0.0 39.1 jit_solution(14724688738438517698)
XLA Ops:
  0.6 0.5 %collective-permute-start = (bf16[72,8192]{1,0:T(8,128)(2,1)}, bf16[72,8192]{1,0:T(8,128)(2,1)S(1)}, u32[]{:S(2)}, u32[]{:S(2)}) collective-permute-start(bf16[72,8192]{1,0:T(8,128)(2,1)} %refs_3_.1), channel_id=1, source_target_pairs={{0,1},{1,0},{2,3},{3,2},{4,5},{5,4},{6,7},{7,6},{8,9},{9,8},{10,11... | collective-permute-start | bytes 3538952 | tf_op jit(solution)/shard_map/ppermute | solution.py:312
  1.1 1.1 %constant_dynamic-slice_fusion = bf16[72,4096]{1,0:T(8,128)(2,1)S(1)} fusion(bf16[72,8192]{1,0:T(8,128)(2,1)} %refs_3_.1, s32[]{:T(128)S(6)} %select_n.48), kind=kLoop, calls=%fused_computation.19 | loop fusion | bytes 1179652 | tf_op jit(solution)/shard_map/dynamic_slice | solution.py:319
  2.3 5.7 %collective-permute-start.1 = (bf16[72,4096]{1,0:T(8,128)(2,1)S(1)}, bf16[72,4096]{1,0:T(8,128)(2,1)S(1)}, u32[]{:S(2)}, u32[]{:S(2)}) collective-permute-start(bf16[72,4096]{1,0:T(8,128)(2,1)S(1)} %constant_dynamic-slice_fusion), channel_id=1, source_target_pairs={{0,15},{1,2},{2,1},{3,4},{4,3},{5,6},{6,5},{7,8},{8,7},{9,10},{10,... | collective-permute-start | bytes 1769480 | tf_op jit(solution)/shard_map/ppermute | solution.py:318
  8.6 0.0 collective-permute-done.refs_4_
  8.6 10.6 %early_tiles.1 = (f32[16,72,128]{2,1,0:T(8,128)S(1)}, bf16[513,128,128]{2,1,0:T(8,128)(2,1)S(1)}, s32[16,128]{1,0:T(8,128)S(1)}, bf16[3,16,128]{2,1,0:T(8,128)(2,1)S(1)}, bf16[3,16,128]{2,1,0:T(8,128)(2,1)S(1)}) custom-call(s32[1]{0:T(128)} %bitcast.4.me, s32[1]{0:T(128)S(6)} %copy.13.count, s32[1,512]{1,0:T(1,128)} %bitcast.13, s32[1,512]{1,0:T(1,128)} %bitcast.14, ...), custom_call_target="tpu_custom_call" | custom-call | flops 1207959552 | bytes 16777216 | tf_op jit(solution)/shard_map/early_tiles/pallas_call | solution.py:338
  19.3 0.0 collective-permute-done.1.far
  19.3 0.0 copy-start.1
  19.3 2.2 %late_tiles.1 = (f32[8,72,128]{2,1,0:T(8,128)S(1)}, bf16[304,128]{1,0:T(8,128)(2,1)S(1)}, bf16[304,128]{1,0:T(8,128)(2,1)S(1)}, bf16[304,128]{1,0:T(8,128)(2,1)S...) custom-call(s32[16,128]{1,0:T(8,128)S(1)} %get-tuple-element.19.meta, ...), custom_call_target="tpu_custom_call" | custom-call | flops 603979776 | bytes 589824 | tf_op jit(solution)/shard_map/late_tiles/pallas_call | solution.py:384
  21.5 0.5 %collective-permute-start.6 = (bf16[304,128]{1,0:T(8,128)(2,1)S(1)}, bf16[304,128]{1,0:T(8,128)(2,1)S(1)}, u32[]{:S(2)}, u32[]{:S(2)}) collective-permute-start(bf16[304,128]{1,0:T(8,128)(2,1)S(1)} %get-tuple-element.31), channel_id=1, source_target_pairs={{0,2},{1,3},{2,0},{3,1},{4,6},{5,7},{6,4},{7,5},{8,10},{9,11},{10,... | collective-permute-start | bytes 233480 | tf_op jit(solution)/shard_map/ppermute | solution.py:312
  22.1 0.0 collective-permute-start.7
  22.1 1.7 %collective-permute-start.8 = (bf16[304,128]{1,0:T(8,128)(2,1)S(1)}, bf16[304,128]{1,0:T(8,128)(2,1)S(1)}, u32[]{:S(2)}, u32[]{:S(2)}) collective-permute-start(bf16[304,128]{1,0:T(8,128)(2,1)S(1)} %get-tuple-element.33), channel_id=1, source_target_pairs={{0,1},{1,0},{2,3},{3,2},{4,5},{5,4},{6,7},{7,6},{8,9},{9,8},{10,11... | collective-permute-start | bytes 233480 | tf_op jit(solution)/shard_map/ppermute | solution.py:312
  23.8 0.5 %collective-permute-start.2 = (bf16[304,128]{1,0:T(8,128)(2,1)S(1)}, bf16[304,128]{1,0:T(8,128)(2,1)S(1)}, u32[]{:S(2)}, u32[]{:S(2)}) collective-permute-start(bf16[304,128]{1,0:T(8,128)(2,1)S(1)} %get-tuple-element.25), channel_id=1, source_target_pairs={{0,2},{1,3},{2,0},{3,1},{4,6},{5,7},{6,4},{7,5},{8,10},{9,11},{10,... | collective-permute-start | bytes 233480 | tf_op jit(solution)/shard_map/ppermute | solution.py:312
  24.2 0.9 %collective-permute-start.3 = (bf16[304,128]{1,0:T(8,128)(2,1)S(1)}, bf16[304,128]{1,0:T(8,128)(2,1)S(1)}, u32[]{:S(2)}, u32[]{:S(2)}) collective-permute-start(bf16[304,128]{1,0:T(8,128)(2,1)S(1)} %get-tuple-element.26), channel_id=1, source_target_pairs={{0,3},{1,2},{2,1},{3,0},{4,7},{5,6},{6,5},{7,4},{8,11},{9,10},{10,... | collective-permute-start | bytes 233480 | tf_op jit(solution)/shard_map/ppermute | solution.py:312
  25.1 1.7 %collective-permute-done.6.refs_0_ = bf16[304,128]{1,0:T(8,128)(2,1)S(1)} collective-permute-done((bf16[304,128]{1,0:T(8,128)(2,1)S(1)}, bf16[304,128]{1,0:T(8,128)(2,1)S(1)}, u32[]{:S(2)}, u32[]{:S(2)}) %collective-permute-start.6) | collective-permute-done | bytes 77856 | tf_op jit(solution)/shard_map/ppermute | solution.py:312
  26.8 0.0 collective-permute-start.4
  26.9 0.0 collective-permute-done.7.refs_1_
  26.9 0.0 collective-permute-done.8.refs_2_
  26.9 0.2 plane_sum.3
  27.0 2.4 %collective-permute-start.10 = (bf16[4,72,128]{2,1,0:T(8,128)(2,1)S(1)}, bf16[4,72,128]{2,1,0:T(8,128)(2,1)S(1)}, u32[]{:S(2)}, u32[]{:S(2)}) collective-permute-start(bf16[4,72,128]{2,1,0:T(8,128)(2,1)S(1)} %get-tuple-element.35), channel_id=1, source_target_pairs={{0,4},{1,5},{2,6},{3,7},{4,8},{5,9},{6,10},{7,11},{8,12},{9,13},{1... | collective-permute-start | bytes 221192 | tf_op jit(solution)/shard_map/ppermute | solution.py:315
  29.5 2.3 %collective-permute-start.9 = (bf16[4,72,128]{2,1,0:T(8,128)(2,1)S(1)}, bf16[4,72,128]{2,1,0:T(8,128)(2,1)S(1)}, u32[]{:S(2)}, u32[]{:S(2)}) collective-permute-start(bf16[4,72,128]{2,1,0:T(8,128)(2,1)S(1)} %get-tuple-element.34), channel_id=1, source_target_pairs={{0,8},{1,9},{2,10},{3,11},{4,12},{5,13},{6,14},{7,15},{8,0},{9,1},... | collective-permute-start | bytes 221192 | tf_op jit(solution)/shard_map/ppermute | solution.py:315
  31.8 0.0 collective-permute-done.2.refs_0_
  31.8 0.0 collective-permute-done.3.refs_1_
  31.8 0.0 collective-permute-done.4.refs_2_
  31.8 0.1 plane_sum.2
  31.9 2.2 %collective-permute-start.5 = (bf16[4,72,128]{2,1,0:T(8,128)(2,1)S(1)}, bf16[4,72,128]{2,1,0:T(8,128)(2,1)S(1)}, u32[]{:S(2)}, u32[]{:S(2)}) collective-permute-start(bf16[4,72,128]{2,1,0:T(8,128)(2,1)S(1)} %get-tuple-element.29), channel_id=1, source_target_pairs={{0,12},{1,13},{2,14},{3,15},{4,0},{5,1},{6,2},{7,3},{8,4},{9,5},{1... | collective-permute-start | bytes 221192 | tf_op jit(solution)/shard_map/ppermute | solution.py:315
  34.1 0.1 fusion.choose
  34.2 0.0 copy-start
  34.2 1.3 %copy.12 = bf16[72,16,1024]{2,0,1:T(8,128)(2,1)S(1)} copy(bf16[72,16,1024]{2,1,0:T(8,128)(2,1)S(1)} %bitcast.12) | data formatting | bytes 4718592 | tf_op jit(solution)/shard_map/reshape | solution.py:375
  35.5 0.0 collective-permute-done.10.refs_3_
  35.5 2.1 %collective-permute-done.9.refs_2_ = bf16[4,72,128]{2,1,0:T(8,128)(2,1)S(1)} collective-permute-done((bf16[4,72,128]{2,1,0:T(8,128)(2,1)S(1)}, bf16[4,72,128]{2,1,0:T(8,128)(2,1)S(1)}, u32[]{:S(2)}, u32[]{:S(2)}) %collective-permute-start.9) | collective-permute-done | bytes 73760 | tf_op jit(solution)/shard_map/ppermute | solution.py:315
  37.6 0.2 collective-permute-done.5.refs_1_
  37.8 1.3 %embed.1 = (bf16[4,72,128]{2,1,0:T(8,128)(2,1)}, bf16[32,1024]{1,0:T(8,128)(2,1)}) custom-call(bf16[128,128]{1,0:T(8,128)(2,1)S(1)} %fusion.choose, bf16[16,72,1024]{2,1,0:T(8,128)(2,1)S(1)} %bitcast.10, f32[1,1024]{1,0:T(1,128)S(1)} %bitcast.11, f32[4,72,128]{2,1,0:T(8,128)S(1)} %get-tuple-element.28.refs_0_, ...), custom_call_target="tpu_custom_call" | custom-call | tf_op jit(solution)/shard_map/embed/pallas_call | solution.py:426
  (3 shorter events, 0.0 us)
Async XLA Ops:
  0.6 8.0 %collective-permute-start = (bf16[72,8192]{1,0:T(8,128)(2,1)}, bf16[72,8192]{1,0:T(8,128)(2,1)S(1)}, u32[]{:S(2)}, u32[]{:S(2)}) collective-permute-start(bf16[72,8192]{1,0:T(8,128)(2,1)} %refs_3_.1), channel_id=1, source_target_pairs={{0,1},{1,0},{2,3},{3,2},{4,5},{5,4},{6,7},{7,6},{8,9},{9,8},{10,11... | collective-permute-start | bytes 3538952 | tf_op jit(solution)/shard_map/ppermute | solution.py:312
  2.3 17.0 %collective-permute-start.1 = (bf16[72,4096]{1,0:T(8,128)(2,1)S(1)}, bf16[72,4096]{1,0:T(8,128)(2,1)S(1)}, u32[]{:S(2)}, u32[]{:S(2)}) collective-permute-start(bf16[72,4096]{1,0:T(8,128)(2,1)S(1)} %constant_dynamic-slice_fusion), channel_id=1, source_target_pairs={{0,15},{1,2},{2,1},{3,4},{4,3},{5,6},{6,5},{7,8},{8,7},{9,10},{10,... | collective-permute-start | bytes 1769480 | tf_op jit(solution)/shard_map/ppermute | solution.py:318
  19.3 14.9 %copy-start.1 = (bf16[1152,1024]{1,0:T(8,128)(2,1)S(1)}, bf16[1152,1024]{1,0:T(8,128)(2,1)}, u32[]{:S(2)}) copy-start(bf16[1152,1024]{1,0:T(8,128)(2,1)} %param.14) | copy-start | bytes 7077892
  21.5 5.3 %collective-permute-start.6 = (bf16[304,128]{1,0:T(8,128)(2,1)S(1)}, bf16[304,128]{1,0:T(8,128)(2,1)S(1)}, u32[]{:S(2)}, u32[]{:S(2)}) collective-permute-start(bf16[304,128]{1,0:T(8,128)(2,1)S(1)} %get-tuple-element.31), channel_id=1, source_target_pairs={{0,2},{1,3},{2,0},{3,1},{4,6},{5,7},{6,4},{7,5},{8,10},{9,11},{10,... | collective-permute-start | bytes 233480 | tf_op jit(solution)/shard_map/ppermute | solution.py:312
  22.1 4.8 %collective-permute-start.7 = (bf16[304,128]{1,0:T(8,128)(2,1)S(1)}, bf16[304,128]{1,0:T(8,128)(2,1)S(1)}, u32[]{:S(2)}, u32[]{:S(2)}) collective-permute-start(bf16[304,128]{1,0:T(8,128)(2,1)S(1)} %get-tuple-element.32), channel_id=1, source_target_pairs={{0,3},{1,2},{2,1},{3,0},{4,7},{5,6},{6,5},{7,4},{8,11},{9,10},{10,... | collective-permute-start | bytes 233480 | tf_op jit(solution)/shard_map/ppermute | solution.py:312
  22.1 4.8 %collective-permute-start.8 = (bf16[304,128]{1,0:T(8,128)(2,1)S(1)}, bf16[304,128]{1,0:T(8,128)(2,1)S(1)}, u32[]{:S(2)}, u32[]{:S(2)}) collective-permute-start(bf16[304,128]{1,0:T(8,128)(2,1)S(1)} %get-tuple-element.33), channel_id=1, source_target_pairs={{0,1},{1,0},{2,3},{3,2},{4,5},{5,4},{6,7},{7,6},{8,9},{9,8},{10,11... | collective-permute-start | bytes 233480 | tf_op jit(solution)/shard_map/ppermute | solution.py:312
  23.8 8.0 %collective-permute-start.2 = (bf16[304,128]{1,0:T(8,128)(2,1)S(1)}, bf16[304,128]{1,0:T(8,128)(2,1)S(1)}, u32[]{:S(2)}, u32[]{:S(2)}) collective-permute-start(bf16[304,128]{1,0:T(8,128)(2,1)S(1)} %get-tuple-element.25), channel_id=1, source_target_pairs={{0,2},{1,3},{2,0},{3,1},{4,6},{5,7},{6,4},{7,5},{8,10},{9,11},{10,... | collective-permute-start | bytes 233480 | tf_op jit(solution)/shard_map/ppermute | solution.py:312
  24.2 7.5 %collective-permute-start.3 = (bf16[304,128]{1,0:T(8,128)(2,1)S(1)}, bf16[304,128]{1,0:T(8,128)(2,1)S(1)}, u32[]{:S(2)}, u32[]{:S(2)}) collective-permute-start(bf16[304,128]{1,0:T(8,128)(2,1)S(1)} %get-tuple-element.26), channel_id=1, source_target_pairs={{0,3},{1,2},{2,1},{3,0},{4,7},{5,6},{6,5},{7,4},{8,11},{9,10},{10,... | collective-permute-start | bytes 233480 | tf_op jit(solution)/shard_map/ppermute | solution.py:312
  26.8 4.9 %collective-permute-start.4 = (bf16[304,128]{1,0:T(8,128)(2,1)S(1)}, bf16[304,128]{1,0:T(8,128)(2,1)S(1)}, u32[]{:S(2)}, u32[]{:S(2)}) collective-permute-start(bf16[304,128]{1,0:T(8,128)(2,1)S(1)} %get-tuple-element.27), channel_id=1, source_target_pairs={{0,1},{1,0},{2,3},{3,2},{4,5},{5,4},{6,7},{7,6},{8,9},{9,8},{10,11... | collective-permute-start | bytes 233480 | tf_op jit(solution)/shard_map/ppermute | solution.py:312
  27.0 8.5 %collective-permute-start.10 = (bf16[4,72,128]{2,1,0:T(8,128)(2,1)S(1)}, bf16[4,72,128]{2,1,0:T(8,128)(2,1)S(1)}, u32[]{:S(2)}, u32[]{:S(2)}) collective-permute-start(bf16[4,72,128]{2,1,0:T(8,128)(2,1)S(1)} %get-tuple-element.35), channel_id=1, source_target_pairs={{0,4},{1,5},{2,6},{3,7},{4,8},{5,9},{6,10},{7,11},{8,12},{9,13},{1... | collective-permute-start | bytes 221192 | tf_op jit(solution)/shard_map/ppermute | solution.py:315
  29.5 8.2 %collective-permute-start.9 = (bf16[4,72,128]{2,1,0:T(8,128)(2,1)S(1)}, bf16[4,72,128]{2,1,0:T(8,128)(2,1)S(1)}, u32[]{:S(2)}, u32[]{:S(2)}) collective-permute-start(bf16[4,72,128]{2,1,0:T(8,128)(2,1)S(1)} %get-tuple-element.34), channel_id=1, source_target_pairs={{0,8},{1,9},{2,10},{3,11},{4,12},{5,13},{6,14},{7,15},{8,0},{9,1},... | collective-permute-start | bytes 221192 | tf_op jit(solution)/shard_map/ppermute | solution.py:315
  31.9 5.9 %collective-permute-start.5 = (bf16[4,72,128]{2,1,0:T(8,128)(2,1)S(1)}, bf16[4,72,128]{2,1,0:T(8,128)(2,1)S(1)}, u32[]{:S(2)}, u32[]{:S(2)}) collective-permute-start(bf16[4,72,128]{2,1,0:T(8,128)(2,1)S(1)} %get-tuple-element.29), channel_id=1, source_target_pairs={{0,12},{1,13},{2,14},{3,15},{4,0},{5,1},{6,2},{7,3},{8,4},{9,5},{1... | collective-permute-start | bytes 221192 | tf_op jit(solution)/shard_map/ppermute | solution.py:315
  34.2 3.6 %copy-start = (f32[1024]{0:T(1024)S(1)}, f32[1024]{0:T(1024)}, u32[]{:S(2)}) copy-start(f32[1024]{0:T(1024)} %param.15) | copy-start | bytes 12292
